TPU v7x, 32 devices: a whole 2x2x4 slice. The times are simulated.
32 devices in a mesh: section: 2 (over x), frames: 4 (over y, core), space: 4 (over z).
Axes of the slice: x: 2, y: 2, z: 4, core: 2. Of those that a mesh axis runs over, the one named last changes fastest.
Arguments:
- base_frames: bfloat16 [8, 32, 32, 8, 128], P(None, 'frames', 'space'), may hold values from -6 to 6
- section_noise: bfloat16 [2, 8, 32, 32, 8, 128], P('section', None, 'frames', 'space'), may hold values from -6 to 6
- noise_levels: bfloat16 [2], P('section'), may hold values from 0.29882812 to 1
- spatial_kernel: bfloat16 [2, 9, 128, 128], P('section'), may hold values from -0.15625 to 0.15625
- temporal_kernel: bfloat16 [2, 3, 128, 128], P('section'), may hold values from -0.15625 to 0.15625
- output_weight: bfloat16 [2, 128, 128], P('section'), may hold values from -0.5 to 0.5
Outputs:
- denoised: bfloat16 [2, 8, 32, 32, 8, 128], P('section', None, 'frames', 'space')
All inputs are finite; a program needn't handle non-finite values.
Results may differ from a plain program's by a relative error of at most 0.008.
Values may be sent and summed in bfloat16 or wider, within the bound.
A program may use at most 64 MiB of HBM per device.

v0:
```python
import jax
import jax.numpy as jnp
from jax import lax
from jax.sharding import PartitionSpec as P


def extended(block, sides, width):
    for axis, dim in sides:
        count = lax.axis_size(axis)
        forward = [(i, i + 1) for i in range(count - 1)]
        backward = [(target, source) for source, target in forward]
        low = lax.ppermute(
            lax.slice_in_dim(block, block.shape[dim] - width, None, axis=dim), axis, forward
        )
        high = lax.ppermute(lax.slice_in_dim(block, 0, width, axis=dim), axis, backward)
        block = jnp.concatenate([low, block, high], axis=dim)
    return block


def from_behind(array, axis, by):
    peers = lax.axis_size(axis)
    pairs = [(i, i + by) for i in range(peers) if 0 <= i + by < peers]
    return lax.ppermute(array, axis, pairs)


def denoise(previous, noise_part, noise_scale, spatial, temporal, out_weight):
    noisy = previous.astype(jnp.float32) + noise_scale * noise_part.astype(jnp.float32)
    normalized = (
        noisy * lax.rsqrt(jnp.mean(noisy * noisy, axis=-1, keepdims=True) + 1e-05)
    ).astype(jnp.bfloat16)
    bordered = extended(normalized, (("frames", 1), ("space", 2)), 1)
    bordered = jnp.pad(bordered, ((0, 0), (0, 0), (0, 0), (1, 1), (0, 0)))
    num_videos, num_frames, num_rows, num_cols, channels = previous.shape
    accumulated = jnp.zeros((num_videos * num_frames * num_rows * num_cols, channels), jnp.float32)
    for tap_index in range(9):
        row_offset = tap_index // 3
        col_offset = tap_index % 3
        shifted_view = bordered[
            :,
            1 : 1 + num_frames,
            row_offset : row_offset + num_rows,
            col_offset : col_offset + num_cols,
            :,
        ]
        accumulated = accumulated + jnp.dot(
            shifted_view.reshape(-1, channels),
            spatial[tap_index],
            preferred_element_type=jnp.float32,
        )
    for tap_index in range(3):
        shifted_view = bordered[
            :, tap_index : tap_index + num_frames, 1 : 1 + num_rows, 1 : 1 + num_cols, :
        ]
        accumulated = accumulated + jnp.dot(
            shifted_view.reshape(-1, channels),
            temporal[tap_index],
            preferred_element_type=jnp.float32,
        )
    activated = jax.nn.silu(accumulated).astype(jnp.bfloat16)
    estimate = jnp.dot(activated, out_weight, preferred_element_type=jnp.float32).reshape(
        previous.shape
    )
    return (noisy - noise_scale * estimate).astype(jnp.bfloat16)


def on_device(
    base_frames, section_noise, noise_levels, spatial_kernel, temporal_kernel, output_weight
):
    section_place = lax.axis_index("section")
    section_count = lax.axis_size("section")
    video_count = base_frames.shape[0]
    own_noise = section_noise[0]
    noise_scale = noise_levels[0].astype(jnp.float32)
    spatial = spatial_kernel[0]
    temporal = temporal_kernel[0]
    out_weight = output_weight[0]

    def advance(step_index, carried):
        received, collected = carried
        member = step_index - section_place
        clipped = jnp.clip(member, 0, video_count - 1)
        own_input = lax.dynamic_slice_in_dim(base_frames, clipped, 1, 0)
        incoming = jnp.where(section_place == 0, own_input, received)
        noise_slice = lax.dynamic_slice_in_dim(own_noise, clipped, 1, 0)
        produced = denoise(incoming, noise_slice, noise_scale, spatial, temporal, out_weight)
        earlier = lax.dynamic_slice_in_dim(collected, clipped, 1, 0)
        usable = jnp.logical_and(member >= 0, member < video_count)
        collected = lax.dynamic_update_slice_in_dim(
            collected, jnp.where(usable, produced, earlier), clipped, 0
        )
        received = from_behind(produced, "section", 1)
        return (received, collected)

    starting = (jnp.zeros_like(base_frames[:1]), jnp.zeros_like(base_frames))
    finished = lax.fori_loop(0, section_count + video_count - 1, advance, starting)
    result = finished[1][None]
    return result


def solution(mesh):
    return jax.shard_map(
        on_device,
        mesh=mesh,
        in_specs=(
            P(None, "frames", "space", None, None),
            P("section", None, "frames", "space", None, None),
            P("section"),
            P("section", None, None, None),
            P("section", None, None, None),
            P("section", None, None),
        ),
        out_specs=P("section", None, "frames", "space", None, None),
        check_vma=False,
    )
```

profile of v0, /device:TPU:30, one launch (start us, length us, event | category | flops | bytes accessed | tf_op | source)
XLA Modules:
  0.0 249.0 jit_solution(17080981367356506814)
XLA Ops:
  1.8 246.2 %while.17 = (s32[]{:T(128)}, bf16[1,8,8,8,128]{4,3,2,1,0:T(8,128)(2,1)S(1)}, bf16[8,8,8,8,128]{4,3,2,1,0:T(8,128)(2,1)S(1)}, pred[]{:T(512)}, s32[]{:T(128)}, /*...) while((s32[]{:T(128)}, ...), condition=%wide.region_2.3_spmd, body=%wide.region_0.2_spmd.sunk | while | flops 223398400 | bytes 13724076 | solution.py:95
  4.0 1.9 collective-permute-start
  6.0 2.4 collective-permute-start.1
  8.4 2.6 %collective-permute-done.1 = bf16[1,1,8,8,128]{4,3,2,1,0:T(8,128)(2,1)S(1)} collective-permute-done((bf16[1,1,8,8,128]{4,3,2,1,0:T(8,128)(2,1)S(1)}, bf16[1,1,8,8,128]{4,3,2,1,0:T(8,128)(2,1)S(1)}, u32[]{:S(2)}, u32[]{:S(2)}) %collective-permute-start.1) | collective-permute-done | bytes 16416 | tf_op jit(solution)/shard_map/while/body/eval_jaxpr/ppermute | solution.py:12
  11.0 2.4 collective-permute-start.2
  13.4 1.3 collective-permute-start.3
  14.9 4.2 %collective-permute-done.3 = bf16[1,10,1,8,128]{4,3,2,1,0:T(8,128)(2,1)S(1)} collective-permute-done((bf16[1,10,1,8,128]{4,3,2,1,0:T(8,128)(2,1)S(1)}, bf16[1,10,1,8,128]{4,3,2,1,0:T(8,128)(2,1)S(1)}, u32[]{:S(2)}, u32[]{:S(2)}) %collective-permute-start.3) | collective-permute-done | bytes 20512 | tf_op jit(solution)/shard_map/while/body/eval_jaxpr/ppermute | solution.py:12
  22.6 1.3 collective-permute-start.4
  23.9 5.6 %collective-permute-done.4 = bf16[1,8,8,8,128]{4,3,2,1,0:T(8,128)(2,1)S(1)} collective-permute-done((bf16[1,8,8,8,128]{4,3,2,1,0:T(8,128)(2,1)S(1)}, bf16[1,8,8,8,128]{4,3,2,1,0:T(8,128)(2,1)S(1)}, u32[]{:S(2)}, u32[]{:S(2)}) %collective-permute-start.4) | collective-permute-done | bytes 131104 | tf_op jit(solution)/shard_map/while/body/eval_jaxpr/ppermute | solution.py:23
  31.7 1.9 collective-permute-start
  33.6 2.4 collective-permute-start.1
  36.0 2.6 %collective-permute-done.1 = bf16[1,1,8,8,128]{4,3,2,1,0:T(8,128)(2,1)S(1)} collective-permute-done((bf16[1,1,8,8,128]{4,3,2,1,0:T(8,128)(2,1)S(1)}, bf16[1,1,8,8,128]{4,3,2,1,0:T(8,128)(2,1)S(1)}, u32[]{:S(2)}, u32[]{:S(2)}) %collective-permute-start.1) | collective-permute-done | bytes 16416 | tf_op jit(solution)/shard_map/while/body/eval_jaxpr/ppermute | solution.py:12
  38.7 2.4 collective-permute-start.2
  41.1 1.3 collective-permute-start.3
  42.5 4.2 %collective-permute-done.3 = bf16[1,10,1,8,128]{4,3,2,1,0:T(8,128)(2,1)S(1)} collective-permute-done((bf16[1,10,1,8,128]{4,3,2,1,0:T(8,128)(2,1)S(1)}, bf16[1,10,1,8,128]{4,3,2,1,0:T(8,128)(2,1)S(1)}, u32[]{:S(2)}, u32[]{:S(2)}) %collective-permute-start.3) | collective-permute-done | bytes 20512 | tf_op jit(solution)/shard_map/while/body/eval_jaxpr/ppermute | solution.py:12
  50.3 1.3 collective-permute-start.4
  51.6 5.6 %collective-permute-done.4 = bf16[1,8,8,8,128]{4,3,2,1,0:T(8,128)(2,1)S(1)} collective-permute-done((bf16[1,8,8,8,128]{4,3,2,1,0:T(8,128)(2,1)S(1)}, bf16[1,8,8,8,128]{4,3,2,1,0:T(8,128)(2,1)S(1)}, u32[]{:S(2)}, u32[]{:S(2)}) %collective-permute-start.4) | collective-permute-done | bytes 131104 | tf_op jit(solution)/shard_map/while/body/eval_jaxpr/ppermute | solution.py:23
  59.3 1.9 collective-permute-start
  61.3 2.4 collective-permute-start.1
  63.7 2.6 %collective-permute-done.1 = bf16[1,1,8,8,128]{4,3,2,1,0:T(8,128)(2,1)S(1)} collective-permute-done((bf16[1,1,8,8,128]{4,3,2,1,0:T(8,128)(2,1)S(1)}, bf16[1,1,8,8,128]{4,3,2,1,0:T(8,128)(2,1)S(1)}, u32[]{:S(2)}, u32[]{:S(2)}) %collective-permute-start.1) | collective-permute-done | bytes 16416 | tf_op jit(solution)/shard_map/while/body/eval_jaxpr/ppermute | solution.py:12
  66.3 2.4 collective-permute-start.2
  68.7 1.3 collective-permute-start.3
  70.2 4.2 %collective-permute-done.3 = bf16[1,10,1,8,128]{4,3,2,1,0:T(8,128)(2,1)S(1)} collective-permute-done((bf16[1,10,1,8,128]{4,3,2,1,0:T(8,128)(2,1)S(1)}, bf16[1,10,1,8,128]{4,3,2,1,0:T(8,128)(2,1)S(1)}, u32[]{:S(2)}, u32[]{:S(2)}) %collective-permute-start.3) | collective-permute-done | bytes 20512 | tf_op jit(solution)/shard_map/while/body/eval_jaxpr/ppermute | solution.py:12
  77.9 1.3 collective-permute-start.4
  79.2 5.6 %collective-permute-done.4 = bf16[1,8,8,8,128]{4,3,2,1,0:T(8,128)(2,1)S(1)} collective-permute-done((bf16[1,8,8,8,128]{4,3,2,1,0:T(8,128)(2,1)S(1)}, bf16[1,8,8,8,128]{4,3,2,1,0:T(8,128)(2,1)S(1)}, u32[]{:S(2)}, u32[]{:S(2)}) %collective-permute-start.4) | collective-permute-done | bytes 131104 | tf_op jit(solution)/shard_map/while/body/eval_jaxpr/ppermute | solution.py:23
  87.0 1.9 collective-permute-start
  88.9 2.4 collective-permute-start.1
  91.3 2.6 %collective-permute-done.1 = bf16[1,1,8,8,128]{4,3,2,1,0:T(8,128)(2,1)S(1)} collective-permute-done((bf16[1,1,8,8,128]{4,3,2,1,0:T(8,128)(2,1)S(1)}, bf16[1,1,8,8,128]{4,3,2,1,0:T(8,128)(2,1)S(1)}, u32[]{:S(2)}, u32[]{:S(2)}) %collective-permute-start.1) | collective-permute-done | bytes 16416 | tf_op jit(solution)/shard_map/while/body/eval_jaxpr/ppermute | solution.py:12
  94.0 1.9 collective-permute-start.2
  95.9 1.3 collective-permute-start.3
  97.4 4.2 %collective-permute-done.3 = bf16[1,10,1,8,128]{4,3,2,1,0:T(8,128)(2,1)S(1)} collective-permute-done((bf16[1,10,1,8,128]{4,3,2,1,0:T(8,128)(2,1)S(1)}, bf16[1,10,1,8,128]{4,3,2,1,0:T(8,128)(2,1)S(1)}, u32[]{:S(2)}, u32[]{:S(2)}) %collective-permute-start.3) | collective-permute-done | bytes 20512 | tf_op jit(solution)/shard_map/while/body/eval_jaxpr/ppermute | solution.py:12
  105.1 1.3 collective-permute-start.4
  106.4 5.6 %collective-permute-done.4 = bf16[1,8,8,8,128]{4,3,2,1,0:T(8,128)(2,1)S(1)} collective-permute-done((bf16[1,8,8,8,128]{4,3,2,1,0:T(8,128)(2,1)S(1)}, bf16[1,8,8,8,128]{4,3,2,1,0:T(8,128)(2,1)S(1)}, u32[]{:S(2)}, u32[]{:S(2)}) %collective-permute-start.4) | collective-permute-done | bytes 131104 | tf_op jit(solution)/shard_map/while/body/eval_jaxpr/ppermute | solution.py:23
  114.2 1.9 collective-permute-start
  116.1 2.4 collective-permute-start.1
  118.5 2.6 %collective-permute-done.1 = bf16[1,1,8,8,128]{4,3,2,1,0:T(8,128)(2,1)S(1)} collective-permute-done((bf16[1,1,8,8,128]{4,3,2,1,0:T(8,128)(2,1)S(1)}, bf16[1,1,8,8,128]{4,3,2,1,0:T(8,128)(2,1)S(1)}, u32[]{:S(2)}, u32[]{:S(2)}) %collective-permute-start.1) | collective-permute-done | bytes 16416 | tf_op jit(solution)/shard_map/while/body/eval_jaxpr/ppermute | solution.py:12
  121.2 1.9 collective-permute-start.2
  124.6 4.2 %collective-permute-done.3 = bf16[1,10,1,8,128]{4,3,2,1,0:T(8,128)(2,1)S(1)} collective-permute-done((bf16[1,10,1,8,128]{4,3,2,1,0:T(8,128)(2,1)S(1)}, bf16[1,10,1,8,128]{4,3,2,1,0:T(8,128)(2,1)S(1)}, u32[]{:S(2)}, u32[]{:S(2)}) %collective-permute-start.3) | collective-permute-done | bytes 20512 | tf_op jit(solution)/shard_map/while/body/eval_jaxpr/ppermute | solution.py:12
  132.3 1.3 collective-permute-start.4
  133.6 5.6 %collective-permute-done.4 = bf16[1,8,8,8,128]{4,3,2,1,0:T(8,128)(2,1)S(1)} collective-permute-done((bf16[1,8,8,8,128]{4,3,2,1,0:T(8,128)(2,1)S(1)}, bf16[1,8,8,8,128]{4,3,2,1,0:T(8,128)(2,1)S(1)}, u32[]{:S(2)}, u32[]{:S(2)}) %collective-permute-start.4) | collective-permute-done | bytes 131104 | tf_op jit(solution)/shard_map/while/body/eval_jaxpr/ppermute | solution.py:23
  141.4 1.9 collective-permute-start
  143.3 2.4 collective-permute-start.1
  145.7 2.6 %collective-permute-done.1 = bf16[1,1,8,8,128]{4,3,2,1,0:T(8,128)(2,1)S(1)} collective-permute-done((bf16[1,1,8,8,128]{4,3,2,1,0:T(8,128)(2,1)S(1)}, bf16[1,1,8,8,128]{4,3,2,1,0:T(8,128)(2,1)S(1)}, u32[]{:S(2)}, u32[]{:S(2)}) %collective-permute-start.1) | collective-permute-done | bytes 16416 | tf_op jit(solution)/shard_map/while/body/eval_jaxpr/ppermute | solution.py:12
  148.4 1.9 collective-permute-start.2
  151.8 4.2 %collective-permute-done.3 = bf16[1,10,1,8,128]{4,3,2,1,0:T(8,128)(2,1)S(1)} collective-permute-done((bf16[1,10,1,8,128]{4,3,2,1,0:T(8,128)(2,1)S(1)}, bf16[1,10,1,8,128]{4,3,2,1,0:T(8,128)(2,1)S(1)}, u32[]{:S(2)}, u32[]{:S(2)}) %collective-permute-start.3) | collective-permute-done | bytes 20512 | tf_op jit(solution)/shard_map/while/body/eval_jaxpr/ppermute | solution.py:12
  160.8 5.6 %collective-permute-done.4 = bf16[1,8,8,8,128]{4,3,2,1,0:T(8,128)(2,1)S(1)} collective-permute-done((bf16[1,8,8,8,128]{4,3,2,1,0:T(8,128)(2,1)S(1)}, bf16[1,8,8,8,128]{4,3,2,1,0:T(8,128)(2,1)S(1)}, u32[]{:S(2)}, u32[]{:S(2)}) %collective-permute-start.4) | collective-permute-done | bytes 131104 | tf_op jit(solution)/shard_map/while/body/eval_jaxpr/ppermute | solution.py:23
  168.6 1.9 collective-permute-start
  170.5 2.4 collective-permute-start.1
  173.0 2.6 %collective-permute-done.1 = bf16[1,1,8,8,128]{4,3,2,1,0:T(8,128)(2,1)S(1)} collective-permute-done((bf16[1,1,8,8,128]{4,3,2,1,0:T(8,128)(2,1)S(1)}, bf16[1,1,8,8,128]{4,3,2,1,0:T(8,128)(2,1)S(1)}, u32[]{:S(2)}, u32[]{:S(2)}) %collective-permute-start.1) | collective-permute-done | bytes 16416 | tf_op jit(solution)/shard_map/while/body/eval_jaxpr/ppermute | solution.py:12
  175.6 1.9 collective-permute-start.2
  179.0 4.2 %collective-permute-done.3 = bf16[1,10,1,8,128]{4,3,2,1,0:T(8,128)(2,1)S(1)} collective-permute-done((bf16[1,10,1,8,128]{4,3,2,1,0:T(8,128)(2,1)S(1)}, bf16[1,10,1,8,128]{4,3,2,1,0:T(8,128)(2,1)S(1)}, u32[]{:S(2)}, u32[]{:S(2)}) %collective-permute-start.3) | collective-permute-done | bytes 20512 | tf_op jit(solution)/shard_map/while/body/eval_jaxpr/ppermute | solution.py:12
  188.0 5.6 %collective-permute-done.4 = bf16[1,8,8,8,128]{4,3,2,1,0:T(8,128)(2,1)S(1)} collective-permute-done((bf16[1,8,8,8,128]{4,3,2,1,0:T(8,128)(2,1)S(1)}, bf16[1,8,8,8,128]{4,3,2,1,0:T(8,128)(2,1)S(1)}, u32[]{:S(2)}, u32[]{:S(2)}) %collective-permute-start.4) | collective-permute-done | bytes 131104 | tf_op jit(solution)/shard_map/while/body/eval_jaxpr/ppermute | solution.py:23
  195.8 1.9 collective-permute-start
  197.7 2.4 collective-permute-start.1
  200.2 2.6 %collective-permute-done.1 = bf16[1,1,8,8,128]{4,3,2,1,0:T(8,128)(2,1)S(1)} collective-permute-done((bf16[1,1,8,8,128]{4,3,2,1,0:T(8,128)(2,1)S(1)}, bf16[1,1,8,8,128]{4,3,2,1,0:T(8,128)(2,1)S(1)}, u32[]{:S(2)}, u32[]{:S(2)}) %collective-permute-start.1) | collective-permute-done | bytes 16416 | tf_op jit(solution)/shard_map/while/body/eval_jaxpr/ppermute | solution.py:12
  202.8 1.9 collective-permute-start.2
  206.2 4.2 %collective-permute-done.3 = bf16[1,10,1,8,128]{4,3,2,1,0:T(8,128)(2,1)S(1)} collective-permute-done((bf16[1,10,1,8,128]{4,3,2,1,0:T(8,128)(2,1)S(1)}, bf16[1,10,1,8,128]{4,3,2,1,0:T(8,128)(2,1)S(1)}, u32[]{:S(2)}, u32[]{:S(2)}) %collective-permute-start.3) | collective-permute-done | bytes 20512 | tf_op jit(solution)/shard_map/while/body/eval_jaxpr/ppermute | solution.py:12
  215.3 5.6 %collective-permute-done.4 = bf16[1,8,8,8,128]{4,3,2,1,0:T(8,128)(2,1)S(1)} collective-permute-done((bf16[1,8,8,8,128]{4,3,2,1,0:T(8,128)(2,1)S(1)}, bf16[1,8,8,8,128]{4,3,2,1,0:T(8,128)(2,1)S(1)}, u32[]{:S(2)}, u32[]{:S(2)}) %collective-permute-start.4) | collective-permute-done | bytes 131104 | tf_op jit(solution)/shard_map/while/body/eval_jaxpr/ppermute | solution.py:23
  223.0 1.9 collective-permute-start
  224.9 2.4 collective-permute-start.1
  227.4 2.6 %collective-permute-done.1 = bf16[1,1,8,8,128]{4,3,2,1,0:T(8,128)(2,1)S(1)} collective-permute-done((bf16[1,1,8,8,128]{4,3,2,1,0:T(8,128)(2,1)S(1)}, bf16[1,1,8,8,128]{4,3,2,1,0:T(8,128)(2,1)S(1)}, u32[]{:S(2)}, u32[]{:S(2)}) %collective-permute-start.1) | collective-permute-done | bytes 16416 | tf_op jit(solution)/shard_map/while/body/eval_jaxpr/ppermute | solution.py:12
  230.0 1.9 collective-permute-start.2
  233.4 4.2 %collective-permute-done.3 = bf16[1,10,1,8,128]{4,3,2,1,0:T(8,128)(2,1)S(1)} collective-permute-done((bf16[1,10,1,8,128]{4,3,2,1,0:T(8,128)(2,1)S(1)}, bf16[1,10,1,8,128]{4,3,2,1,0:T(8,128)(2,1)S(1)}, u32[]{:S(2)}, u32[]{:S(2)}) %collective-permute-start.3) | collective-permute-done | bytes 20512 | tf_op jit(solution)/shard_map/while/body/eval_jaxpr/ppermute | solution.py:12
  242.5 5.6 %collective-permute-done.4 = bf16[1,8,8,8,128]{4,3,2,1,0:T(8,128)(2,1)S(1)} collective-permute-done((bf16[1,8,8,8,128]{4,3,2,1,0:T(8,128)(2,1)S(1)}, bf16[1,8,8,8,128]{4,3,2,1,0:T(8,128)(2,1)S(1)}, u32[]{:S(2)}, u32[]{:S(2)}) %collective-permute-start.4) | collective-permute-done | bytes 131104 | tf_op jit(solution)/shard_map/while/body/eval_jaxpr/ppermute | solution.py:23
  (226 shorter events, 65.8 us)
Async XLA Ops:
  0.7 1.0 copy-start
  0.9 0.9 copy-start.2
  0.9 0.9 copy-start.3
  4.0 4.3 %collective-permute-start = (bf16[1,1,8,8,128]{4,3,2,1,0:T(8,128)(2,1)S(1)}, bf16[1,1,8,8,128]{4,3,2,1,0:T(8,128)(2,1)S(1)}, u32[]{:S(2)}, u32[]{:S(2)}) collective-permute-start(bf16[1,1,8,8,128]{4,3,2,1,0:T(8,128)(2,1)S(1)} %get-tuple-element.381), channel_id=1, source_target_pairs={{4,0},{8,4},{12,8},{5,1},{9,5},{13,9},{6,2},{10,6},{14,10},{7,3},{... | collective-permute-start | bytes 49160 | tf_op jit(solution)/shard_map/while/body/eval_jaxpr/ppermute | solution.py:15
  6.0 5.1 %collective-permute-start.1 = (bf16[1,1,8,8,128]{4,3,2,1,0:T(8,128)(2,1)S(1)}, bf16[1,1,8,8,128]{4,3,2,1,0:T(8,128)(2,1)S(1)}, u32[]{:S(2)}, u32[]{:S(2)}) collective-permute-start(bf16[1,1,8,8,128]{4,3,2,1,0:T(8,128)(2,1)S(1)} %get-tuple-element.382), channel_id=1, source_target_pairs={{0,4},{4,8},{8,12},{1,5},{5,9},{9,13},{2,6},{6,10},{10,14},{3,7},{... | collective-permute-start | bytes 49160 | tf_op jit(solution)/shard_map/while/body/eval_jaxpr/ppermute | solution.py:12
  11.0 3.8 %collective-permute-start.2 = (bf16[1,10,1,8,128]{4,3,2,1,0:T(8,128)(2,1)S(1)}, bf16[1,10,1,8,128]{4,3,2,1,0:T(8,128)(2,1)S(1)}, u32[]{:S(2)}, u32[]{:S(2)}) collective-permute-start(bf16[1,10,1,8,128]{4,3,2,1,0:T(8,128)(2,1)S(1)} %get-tuple-element.383), channel_id=1, source_target_pairs={{1,0},{2,1},{3,2},{5,4},{6,5},{7,6},{9,8},{10,9},{11,10},{13,12},{... | collective-permute-start | bytes 61448 | tf_op jit(solution)/shard_map/while/body/eval_jaxpr/ppermute | solution.py:15
  13.4 5.7 %collective-permute-start.3 = (bf16[1,10,1,8,128]{4,3,2,1,0:T(8,128)(2,1)S(1)}, bf16[1,10,1,8,128]{4,3,2,1,0:T(8,128)(2,1)S(1)}, u32[]{:S(2)}, u32[]{:S(2)}) collective-permute-start(bf16[1,10,1,8,128]{4,3,2,1,0:T(8,128)(2,1)S(1)} %get-tuple-element.384), channel_id=1, source_target_pairs={{0,1},{1,2},{2,3},{4,5},{5,6},{6,7},{8,9},{9,10},{10,11},{12,13},{... | collective-permute-start | bytes 61448 | tf_op jit(solution)/shard_map/while/body/eval_jaxpr/ppermute | solution.py:12
  22.6 6.9 %collective-permute-start.4 = (bf16[1,8,8,8,128]{4,3,2,1,0:T(8,128)(2,1)S(1)}, bf16[1,8,8,8,128]{4,3,2,1,0:T(8,128)(2,1)S(1)}, u32[]{:S(2)}, u32[]{:S(2)}) collective-permute-start(bf16[1,8,8,8,128]{4,3,2,1,0:T(8,128)(2,1)S(1)} %get-tuple-element.395), channel_id=1, source_target_pairs={{0,16},{1,17},{2,18},{3,19},{4,20},{5,21},{6,22},{7,23},{8,24},{9,... | collective-permute-start | bytes 393224 | tf_op jit(solution)/shard_map/while/body/eval_jaxpr/ppermute | solution.py:23
  31.7 4.3 %collective-permute-start = (bf16[1,1,8,8,128]{4,3,2,1,0:T(8,128)(2,1)S(1)}, bf16[1,1,8,8,128]{4,3,2,1,0:T(8,128)(2,1)S(1)}, u32[]{:S(2)}, u32[]{:S(2)}) collective-permute-start(bf16[1,1,8,8,128]{4,3,2,1,0:T(8,128)(2,1)S(1)} %get-tuple-element.381), channel_id=1, source_target_pairs={{4,0},{8,4},{12,8},{5,1},{9,5},{13,9},{6,2},{10,6},{14,10},{7,3},{... | collective-permute-start | bytes 49160 | tf_op jit(solution)/shard_map/while/body/eval_jaxpr/ppermute | solution.py:15
  33.6 5.1 %collective-permute-start.1 = (bf16[1,1,8,8,128]{4,3,2,1,0:T(8,128)(2,1)S(1)}, bf16[1,1,8,8,128]{4,3,2,1,0:T(8,128)(2,1)S(1)}, u32[]{:S(2)}, u32[]{:S(2)}) collective-permute-start(bf16[1,1,8,8,128]{4,3,2,1,0:T(8,128)(2,1)S(1)} %get-tuple-element.382), channel_id=1, source_target_pairs={{0,4},{4,8},{8,12},{1,5},{5,9},{9,13},{2,6},{6,10},{10,14},{3,7},{... | collective-permute-start | bytes 49160 | tf_op jit(solution)/shard_map/while/body/eval_jaxpr/ppermute | solution.py:12
  38.7 3.9 %collective-permute-start.2 = (bf16[1,10,1,8,128]{4,3,2,1,0:T(8,128)(2,1)S(1)}, bf16[1,10,1,8,128]{4,3,2,1,0:T(8,128)(2,1)S(1)}, u32[]{:S(2)}, u32[]{:S(2)}) collective-permute-start(bf16[1,10,1,8,128]{4,3,2,1,0:T(8,128)(2,1)S(1)} %get-tuple-element.383), channel_id=1, source_target_pairs={{1,0},{2,1},{3,2},{5,4},{6,5},{7,6},{9,8},{10,9},{11,10},{13,12},{... | collective-permute-start | bytes 61448 | tf_op jit(solution)/shard_map/while/body/eval_jaxpr/ppermute | solution.py:15
  41.1 5.7 %collective-permute-start.3 = (bf16[1,10,1,8,128]{4,3,2,1,0:T(8,128)(2,1)S(1)}, bf16[1,10,1,8,128]{4,3,2,1,0:T(8,128)(2,1)S(1)}, u32[]{:S(2)}, u32[]{:S(2)}) collective-permute-start(bf16[1,10,1,8,128]{4,3,2,1,0:T(8,128)(2,1)S(1)} %get-tuple-element.384), channel_id=1, source_target_pairs={{0,1},{1,2},{2,3},{4,5},{5,6},{6,7},{8,9},{9,10},{10,11},{12,13},{... | collective-permute-start | bytes 61448 | tf_op jit(solution)/shard_map/while/body/eval_jaxpr/ppermute | solution.py:12
  50.3 6.9 %collective-permute-start.4 = (bf16[1,8,8,8,128]{4,3,2,1,0:T(8,128)(2,1)S(1)}, bf16[1,8,8,8,128]{4,3,2,1,0:T(8,128)(2,1)S(1)}, u32[]{:S(2)}, u32[]{:S(2)}) collective-permute-start(bf16[1,8,8,8,128]{4,3,2,1,0:T(8,128)(2,1)S(1)} %get-tuple-element.395), channel_id=1, source_target_pairs={{0,16},{1,17},{2,18},{3,19},{4,20},{5,21},{6,22},{7,23},{8,24},{9,... | collective-permute-start | bytes 393224 | tf_op jit(solution)/shard_map/while/body/eval_jaxpr/ppermute | solution.py:23
  59.3 4.3 %collective-permute-start = (bf16[1,1,8,8,128]{4,3,2,1,0:T(8,128)(2,1)S(1)}, bf16[1,1,8,8,128]{4,3,2,1,0:T(8,128)(2,1)S(1)}, u32[]{:S(2)}, u32[]{:S(2)}) collective-permute-start(bf16[1,1,8,8,128]{4,3,2,1,0:T(8,128)(2,1)S(1)} %get-tuple-element.381), channel_id=1, source_target_pairs={{4,0},{8,4},{12,8},{5,1},{9,5},{13,9},{6,2},{10,6},{14,10},{7,3},{... | collective-permute-start | bytes 49160 | tf_op jit(solution)/shard_map/while/body/eval_jaxpr/ppermute | solution.py:15
  61.3 5.1 %collective-permute-start.1 = (bf16[1,1,8,8,128]{4,3,2,1,0:T(8,128)(2,1)S(1)}, bf16[1,1,8,8,128]{4,3,2,1,0:T(8,128)(2,1)S(1)}, u32[]{:S(2)}, u32[]{:S(2)}) collective-permute-start(bf16[1,1,8,8,128]{4,3,2,1,0:T(8,128)(2,1)S(1)} %get-tuple-element.382), channel_id=1, source_target_pairs={{0,4},{4,8},{8,12},{1,5},{5,9},{9,13},{2,6},{6,10},{10,14},{3,7},{... | collective-permute-start | bytes 49160 | tf_op jit(solution)/shard_map/while/body/eval_jaxpr/ppermute | solution.py:12
  66.3 3.9 %collective-permute-start.2 = (bf16[1,10,1,8,128]{4,3,2,1,0:T(8,128)(2,1)S(1)}, bf16[1,10,1,8,128]{4,3,2,1,0:T(8,128)(2,1)S(1)}, u32[]{:S(2)}, u32[]{:S(2)}) collective-permute-start(bf16[1,10,1,8,128]{4,3,2,1,0:T(8,128)(2,1)S(1)} %get-tuple-element.383), channel_id=1, source_target_pairs={{1,0},{2,1},{3,2},{5,4},{6,5},{7,6},{9,8},{10,9},{11,10},{13,12},{... | collective-permute-start | bytes 61448 | tf_op jit(solution)/shard_map/while/body/eval_jaxpr/ppermute | solution.py:15
  68.7 5.7 %collective-permute-start.3 = (bf16[1,10,1,8,128]{4,3,2,1,0:T(8,128)(2,1)S(1)}, bf16[1,10,1,8,128]{4,3,2,1,0:T(8,128)(2,1)S(1)}, u32[]{:S(2)}, u32[]{:S(2)}) collective-permute-start(bf16[1,10,1,8,128]{4,3,2,1,0:T(8,128)(2,1)S(1)} %get-tuple-element.384), channel_id=1, source_target_pairs={{0,1},{1,2},{2,3},{4,5},{5,6},{6,7},{8,9},{9,10},{10,11},{12,13},{... | collective-permute-start | bytes 61448 | tf_op jit(solution)/shard_map/while/body/eval_jaxpr/ppermute | solution.py:12
  77.9 6.9 %collective-permute-start.4 = (bf16[1,8,8,8,128]{4,3,2,1,0:T(8,128)(2,1)S(1)}, bf16[1,8,8,8,128]{4,3,2,1,0:T(8,128)(2,1)S(1)}, u32[]{:S(2)}, u32[]{:S(2)}) collective-permute-start(bf16[1,8,8,8,128]{4,3,2,1,0:T(8,128)(2,1)S(1)} %get-tuple-element.395), channel_id=1, source_target_pairs={{0,16},{1,17},{2,18},{3,19},{4,20},{5,21},{6,22},{7,23},{8,24},{9,... | collective-permute-start | bytes 393224 | tf_op jit(solution)/shard_map/while/body/eval_jaxpr/ppermute | solution.py:23
  87.0 4.3 %collective-permute-start = (bf16[1,1,8,8,128]{4,3,2,1,0:T(8,128)(2,1)S(1)}, bf16[1,1,8,8,128]{4,3,2,1,0:T(8,128)(2,1)S(1)}, u32[]{:S(2)}, u32[]{:S(2)}) collective-permute-start(bf16[1,1,8,8,128]{4,3,2,1,0:T(8,128)(2,1)S(1)} %get-tuple-element.381), channel_id=1, source_target_pairs={{4,0},{8,4},{12,8},{5,1},{9,5},{13,9},{6,2},{10,6},{14,10},{7,3},{... | collective-permute-start | bytes 49160 | tf_op jit(solution)/shard_map/while/body/eval_jaxpr/ppermute | solution.py:15
  88.9 5.1 %collective-permute-start.1 = (bf16[1,1,8,8,128]{4,3,2,1,0:T(8,128)(2,1)S(1)}, bf16[1,1,8,8,128]{4,3,2,1,0:T(8,128)(2,1)S(1)}, u32[]{:S(2)}, u32[]{:S(2)}) collective-permute-start(bf16[1,1,8,8,128]{4,3,2,1,0:T(8,128)(2,1)S(1)} %get-tuple-element.382), channel_id=1, source_target_pairs={{0,4},{4,8},{8,12},{1,5},{5,9},{9,13},{2,6},{6,10},{10,14},{3,7},{... | collective-permute-start | bytes 49160 | tf_op jit(solution)/shard_map/while/body/eval_jaxpr/ppermute | solution.py:12
  94.0 3.4 %collective-permute-start.2 = (bf16[1,10,1,8,128]{4,3,2,1,0:T(8,128)(2,1)S(1)}, bf16[1,10,1,8,128]{4,3,2,1,0:T(8,128)(2,1)S(1)}, u32[]{:S(2)}, u32[]{:S(2)}) collective-permute-start(bf16[1,10,1,8,128]{4,3,2,1,0:T(8,128)(2,1)S(1)} %get-tuple-element.383), channel_id=1, source_target_pairs={{1,0},{2,1},{3,2},{5,4},{6,5},{7,6},{9,8},{10,9},{11,10},{13,12},{... | collective-permute-start | bytes 61448 | tf_op jit(solution)/shard_map/while/body/eval_jaxpr/ppermute | solution.py:15
  95.9 5.7 %collective-permute-start.3 = (bf16[1,10,1,8,128]{4,3,2,1,0:T(8,128)(2,1)S(1)}, bf16[1,10,1,8,128]{4,3,2,1,0:T(8,128)(2,1)S(1)}, u32[]{:S(2)}, u32[]{:S(2)}) collective-permute-start(bf16[1,10,1,8,128]{4,3,2,1,0:T(8,128)(2,1)S(1)} %get-tuple-element.384), channel_id=1, source_target_pairs={{0,1},{1,2},{2,3},{4,5},{5,6},{6,7},{8,9},{9,10},{10,11},{12,13},{... | collective-permute-start | bytes 61448 | tf_op jit(solution)/shard_map/while/body/eval_jaxpr/ppermute | solution.py:12
  105.1 6.9 %collective-permute-start.4 = (bf16[1,8,8,8,128]{4,3,2,1,0:T(8,128)(2,1)S(1)}, bf16[1,8,8,8,128]{4,3,2,1,0:T(8,128)(2,1)S(1)}, u32[]{:S(2)}, u32[]{:S(2)}) collective-permute-start(bf16[1,8,8,8,128]{4,3,2,1,0:T(8,128)(2,1)S(1)} %get-tuple-element.395), channel_id=1, source_target_pairs={{0,16},{1,17},{2,18},{3,19},{4,20},{5,21},{6,22},{7,23},{8,24},{9,... | collective-permute-start | bytes 393224 | tf_op jit(solution)/shard_map/while/body/eval_jaxpr/ppermute | solution.py:23
  114.2 4.3 %collective-permute-start = (bf16[1,1,8,8,128]{4,3,2,1,0:T(8,128)(2,1)S(1)}, bf16[1,1,8,8,128]{4,3,2,1,0:T(8,128)(2,1)S(1)}, u32[]{:S(2)}, u32[]{:S(2)}) collective-permute-start(bf16[1,1,8,8,128]{4,3,2,1,0:T(8,128)(2,1)S(1)} %get-tuple-element.381), channel_id=1, source_target_pairs={{4,0},{8,4},{12,8},{5,1},{9,5},{13,9},{6,2},{10,6},{14,10},{7,3},{... | collective-permute-start | bytes 49160 | tf_op jit(solution)/shard_map/while/body/eval_jaxpr/ppermute | solution.py:15
  116.1 5.1 %collective-permute-start.1 = (bf16[1,1,8,8,128]{4,3,2,1,0:T(8,128)(2,1)S(1)}, bf16[1,1,8,8,128]{4,3,2,1,0:T(8,128)(2,1)S(1)}, u32[]{:S(2)}, u32[]{:S(2)}) collective-permute-start(bf16[1,1,8,8,128]{4,3,2,1,0:T(8,128)(2,1)S(1)} %get-tuple-element.382), channel_id=1, source_target_pairs={{0,4},{4,8},{8,12},{1,5},{5,9},{9,13},{2,6},{6,10},{10,14},{3,7},{... | collective-permute-start | bytes 49160 | tf_op jit(solution)/shard_map/while/body/eval_jaxpr/ppermute | solution.py:12
  121.2 3.4 %collective-permute-start.2 = (bf16[1,10,1,8,128]{4,3,2,1,0:T(8,128)(2,1)S(1)}, bf16[1,10,1,8,128]{4,3,2,1,0:T(8,128)(2,1)S(1)}, u32[]{:S(2)}, u32[]{:S(2)}) collective-permute-start(bf16[1,10,1,8,128]{4,3,2,1,0:T(8,128)(2,1)S(1)} %get-tuple-element.383), channel_id=1, source_target_pairs={{1,0},{2,1},{3,2},{5,4},{6,5},{7,6},{9,8},{10,9},{11,10},{13,12},{... | collective-permute-start | bytes 61448 | tf_op jit(solution)/shard_map/while/body/eval_jaxpr/ppermute | solution.py:15
  123.1 5.7 %collective-permute-start.3 = (bf16[1,10,1,8,128]{4,3,2,1,0:T(8,128)(2,1)S(1)}, bf16[1,10,1,8,128]{4,3,2,1,0:T(8,128)(2,1)S(1)}, u32[]{:S(2)}, u32[]{:S(2)}) collective-permute-start(bf16[1,10,1,8,128]{4,3,2,1,0:T(8,128)(2,1)S(1)} %get-tuple-element.384), channel_id=1, source_target_pairs={{0,1},{1,2},{2,3},{4,5},{5,6},{6,7},{8,9},{9,10},{10,11},{12,13},{... | collective-permute-start | bytes 61448 | tf_op jit(solution)/shard_map/while/body/eval_jaxpr/ppermute | solution.py:12
  132.3 6.9 %collective-permute-start.4 = (bf16[1,8,8,8,128]{4,3,2,1,0:T(8,128)(2,1)S(1)}, bf16[1,8,8,8,128]{4,3,2,1,0:T(8,128)(2,1)S(1)}, u32[]{:S(2)}, u32[]{:S(2)}) collective-permute-start(bf16[1,8,8,8,128]{4,3,2,1,0:T(8,128)(2,1)S(1)} %get-tuple-element.395), channel_id=1, source_target_pairs={{0,16},{1,17},{2,18},{3,19},{4,20},{5,21},{6,22},{7,23},{8,24},{9,... | collective-permute-start | bytes 393224 | tf_op jit(solution)/shard_map/while/body/eval_jaxpr/ppermute | solution.py:23
  141.4 4.3 %collective-permute-start = (bf16[1,1,8,8,128]{4,3,2,1,0:T(8,128)(2,1)S(1)}, bf16[1,1,8,8,128]{4,3,2,1,0:T(8,128)(2,1)S(1)}, u32[]{:S(2)}, u32[]{:S(2)}) collective-permute-start(bf16[1,1,8,8,128]{4,3,2,1,0:T(8,128)(2,1)S(1)} %get-tuple-element.381), channel_id=1, source_target_pairs={{4,0},{8,4},{12,8},{5,1},{9,5},{13,9},{6,2},{10,6},{14,10},{7,3},{... | collective-permute-start | bytes 49160 | tf_op jit(solution)/shard_map/while/body/eval_jaxpr/ppermute | solution.py:15
  143.3 5.1 %collective-permute-start.1 = (bf16[1,1,8,8,128]{4,3,2,1,0:T(8,128)(2,1)S(1)}, bf16[1,1,8,8,128]{4,3,2,1,0:T(8,128)(2,1)S(1)}, u32[]{:S(2)}, u32[]{:S(2)}) collective-permute-start(bf16[1,1,8,8,128]{4,3,2,1,0:T(8,128)(2,1)S(1)} %get-tuple-element.382), channel_id=1, source_target_pairs={{0,4},{4,8},{8,12},{1,5},{5,9},{9,13},{2,6},{6,10},{10,14},{3,7},{... | collective-permute-start | bytes 49160 | tf_op jit(solution)/shard_map/while/body/eval_jaxpr/ppermute | solution.py:12
  148.4 3.4 %collective-permute-start.2 = (bf16[1,10,1,8,128]{4,3,2,1,0:T(8,128)(2,1)S(1)}, bf16[1,10,1,8,128]{4,3,2,1,0:T(8,128)(2,1)S(1)}, u32[]{:S(2)}, u32[]{:S(2)}) collective-permute-start(bf16[1,10,1,8,128]{4,3,2,1,0:T(8,128)(2,1)S(1)} %get-tuple-element.383), channel_id=1, source_target_pairs={{1,0},{2,1},{3,2},{5,4},{6,5},{7,6},{9,8},{10,9},{11,10},{13,12},{... | collective-permute-start | bytes 61448 | tf_op jit(solution)/shard_map/while/body/eval_jaxpr/ppermute | solution.py:15
  150.3 5.7 %collective-permute-start.3 = (bf16[1,10,1,8,128]{4,3,2,1,0:T(8,128)(2,1)S(1)}, bf16[1,10,1,8,128]{4,3,2,1,0:T(8,128)(2,1)S(1)}, u32[]{:S(2)}, u32[]{:S(2)}) collective-permute-start(bf16[1,10,1,8,128]{4,3,2,1,0:T(8,128)(2,1)S(1)} %get-tuple-element.384), channel_id=1, source_target_pairs={{0,1},{1,2},{2,3},{4,5},{5,6},{6,7},{8,9},{9,10},{10,11},{12,13},{... | collective-permute-start | bytes 61448 | tf_op jit(solution)/shard_map/while/body/eval_jaxpr/ppermute | solution.py:12
  159.5 6.9 %collective-permute-start.4 = (bf16[1,8,8,8,128]{4,3,2,1,0:T(8,128)(2,1)S(1)}, bf16[1,8,8,8,128]{4,3,2,1,0:T(8,128)(2,1)S(1)}, u32[]{:S(2)}, u32[]{:S(2)}) collective-permute-start(bf16[1,8,8,8,128]{4,3,2,1,0:T(8,128)(2,1)S(1)} %get-tuple-element.395), channel_id=1, source_target_pairs={{0,16},{1,17},{2,18},{3,19},{4,20},{5,21},{6,22},{7,23},{8,24},{9,... | collective-permute-start | bytes 393224 | tf_op jit(solution)/shard_map/while/body/eval_jaxpr/ppermute | solution.py:23
  168.6 4.3 %collective-permute-start = (bf16[1,1,8,8,128]{4,3,2,1,0:T(8,128)(2,1)S(1)}, bf16[1,1,8,8,128]{4,3,2,1,0:T(8,128)(2,1)S(1)}, u32[]{:S(2)}, u32[]{:S(2)}) collective-permute-start(bf16[1,1,8,8,128]{4,3,2,1,0:T(8,128)(2,1)S(1)} %get-tuple-element.381), channel_id=1, source_target_pairs={{4,0},{8,4},{12,8},{5,1},{9,5},{13,9},{6,2},{10,6},{14,10},{7,3},{... | collective-permute-start | bytes 49160 | tf_op jit(solution)/shard_map/while/body/eval_jaxpr/ppermute | solution.py:15
  170.5 5.1 %collective-permute-start.1 = (bf16[1,1,8,8,128]{4,3,2,1,0:T(8,128)(2,1)S(1)}, bf16[1,1,8,8,128]{4,3,2,1,0:T(8,128)(2,1)S(1)}, u32[]{:S(2)}, u32[]{:S(2)}) collective-permute-start(bf16[1,1,8,8,128]{4,3,2,1,0:T(8,128)(2,1)S(1)} %get-tuple-element.382), channel_id=1, source_target_pairs={{0,4},{4,8},{8,12},{1,5},{5,9},{9,13},{2,6},{6,10},{10,14},{3,7},{... | collective-permute-start | bytes 49160 | tf_op jit(solution)/shard_map/while/body/eval_jaxpr/ppermute | solution.py:12
  175.6 3.4 %collective-permute-start.2 = (bf16[1,10,1,8,128]{4,3,2,1,0:T(8,128)(2,1)S(1)}, bf16[1,10,1,8,128]{4,3,2,1,0:T(8,128)(2,1)S(1)}, u32[]{:S(2)}, u32[]{:S(2)}) collective-permute-start(bf16[1,10,1,8,128]{4,3,2,1,0:T(8,128)(2,1)S(1)} %get-tuple-element.383), channel_id=1, source_target_pairs={{1,0},{2,1},{3,2},{5,4},{6,5},{7,6},{9,8},{10,9},{11,10},{13,12},{... | collective-permute-start | bytes 61448 | tf_op jit(solution)/shard_map/while/body/eval_jaxpr/ppermute | solution.py:15
  177.5 5.7 %collective-permute-start.3 = (bf16[1,10,1,8,128]{4,3,2,1,0:T(8,128)(2,1)S(1)}, bf16[1,10,1,8,128]{4,3,2,1,0:T(8,128)(2,1)S(1)}, u32[]{:S(2)}, u32[]{:S(2)}) collective-permute-start(bf16[1,10,1,8,128]{4,3,2,1,0:T(8,128)(2,1)S(1)} %get-tuple-element.384), channel_id=1, source_target_pairs={{0,1},{1,2},{2,3},{4,5},{5,6},{6,7},{8,9},{9,10},{10,11},{12,13},{... | collective-permute-start | bytes 61448 | tf_op jit(solution)/shard_map/while/body/eval_jaxpr/ppermute | solution.py:12
  186.7 6.9 %collective-permute-start.4 = (bf16[1,8,8,8,128]{4,3,2,1,0:T(8,128)(2,1)S(1)}, bf16[1,8,8,8,128]{4,3,2,1,0:T(8,128)(2,1)S(1)}, u32[]{:S(2)}, u32[]{:S(2)}) collective-permute-start(bf16[1,8,8,8,128]{4,3,2,1,0:T(8,128)(2,1)S(1)} %get-tuple-element.395), channel_id=1, source_target_pairs={{0,16},{1,17},{2,18},{3,19},{4,20},{5,21},{6,22},{7,23},{8,24},{9,... | collective-permute-start | bytes 393224 | tf_op jit(solution)/shard_map/while/body/eval_jaxpr/ppermute | solution.py:23
  195.8 4.3 %collective-permute-start = (bf16[1,1,8,8,128]{4,3,2,1,0:T(8,128)(2,1)S(1)}, bf16[1,1,8,8,128]{4,3,2,1,0:T(8,128)(2,1)S(1)}, u32[]{:S(2)}, u32[]{:S(2)}) collective-permute-start(bf16[1,1,8,8,128]{4,3,2,1,0:T(8,128)(2,1)S(1)} %get-tuple-element.381), channel_id=1, source_target_pairs={{4,0},{8,4},{12,8},{5,1},{9,5},{13,9},{6,2},{10,6},{14,10},{7,3},{... | collective-permute-start | bytes 49160 | tf_op jit(solution)/shard_map/while/body/eval_jaxpr/ppermute | solution.py:15
  197.7 5.1 %collective-permute-start.1 = (bf16[1,1,8,8,128]{4,3,2,1,0:T(8,128)(2,1)S(1)}, bf16[1,1,8,8,128]{4,3,2,1,0:T(8,128)(2,1)S(1)}, u32[]{:S(2)}, u32[]{:S(2)}) collective-permute-start(bf16[1,1,8,8,128]{4,3,2,1,0:T(8,128)(2,1)S(1)} %get-tuple-element.382), channel_id=1, source_target_pairs={{0,4},{4,8},{8,12},{1,5},{5,9},{9,13},{2,6},{6,10},{10,14},{3,7},{... | collective-permute-start | bytes 49160 | tf_op jit(solution)/shard_map/while/body/eval_jaxpr/ppermute | solution.py:12
  202.8 3.4 %collective-permute-start.2 = (bf16[1,10,1,8,128]{4,3,2,1,0:T(8,128)(2,1)S(1)}, bf16[1,10,1,8,128]{4,3,2,1,0:T(8,128)(2,1)S(1)}, u32[]{:S(2)}, u32[]{:S(2)}) collective-permute-start(bf16[1,10,1,8,128]{4,3,2,1,0:T(8,128)(2,1)S(1)} %get-tuple-element.383), channel_id=1, source_target_pairs={{1,0},{2,1},{3,2},{5,4},{6,5},{7,6},{9,8},{10,9},{11,10},{13,12},{... | collective-permute-start | bytes 61448 | tf_op jit(solution)/shard_map/while/body/eval_jaxpr/ppermute | solution.py:15
  204.7 5.7 %collective-permute-start.3 = (bf16[1,10,1,8,128]{4,3,2,1,0:T(8,128)(2,1)S(1)}, bf16[1,10,1,8,128]{4,3,2,1,0:T(8,128)(2,1)S(1)}, u32[]{:S(2)}, u32[]{:S(2)}) collective-permute-start(bf16[1,10,1,8,128]{4,3,2,1,0:T(8,128)(2,1)S(1)} %get-tuple-element.384), channel_id=1, source_target_pairs={{0,1},{1,2},{2,3},{4,5},{5,6},{6,7},{8,9},{9,10},{10,11},{12,13},{... | collective-permute-start | bytes 61448 | tf_op jit(solution)/shard_map/while/body/eval_jaxpr/ppermute | solution.py:12
  213.9 6.9 %collective-permute-start.4 = (bf16[1,8,8,8,128]{4,3,2,1,0:T(8,128)(2,1)S(1)}, bf16[1,8,8,8,128]{4,3,2,1,0:T(8,128)(2,1)S(1)}, u32[]{:S(2)}, u32[]{:S(2)}) collective-permute-start(bf16[1,8,8,8,128]{4,3,2,1,0:T(8,128)(2,1)S(1)} %get-tuple-element.395), channel_id=1, source_target_pairs={{0,16},{1,17},{2,18},{3,19},{4,20},{5,21},{6,22},{7,23},{8,24},{9,... | collective-permute-start | bytes 393224 | tf_op jit(solution)/shard_map/while/body/eval_jaxpr/ppermute | solution.py:23
  223.0 4.3 %collective-permute-start = (bf16[1,1,8,8,128]{4,3,2,1,0:T(8,128)(2,1)S(1)}, bf16[1,1,8,8,128]{4,3,2,1,0:T(8,128)(2,1)S(1)}, u32[]{:S(2)}, u32[]{:S(2)}) collective-permute-start(bf16[1,1,8,8,128]{4,3,2,1,0:T(8,128)(2,1)S(1)} %get-tuple-element.381), channel_id=1, source_target_pairs={{4,0},{8,4},{12,8},{5,1},{9,5},{13,9},{6,2},{10,6},{14,10},{7,3},{... | collective-permute-start | bytes 49160 | tf_op jit(solution)/shard_map/while/body/eval_jaxpr/ppermute | solution.py:15
  224.9 5.1 %collective-permute-start.1 = (bf16[1,1,8,8,128]{4,3,2,1,0:T(8,128)(2,1)S(1)}, bf16[1,1,8,8,128]{4,3,2,1,0:T(8,128)(2,1)S(1)}, u32[]{:S(2)}, u32[]{:S(2)}) collective-permute-start(bf16[1,1,8,8,128]{4,3,2,1,0:T(8,128)(2,1)S(1)} %get-tuple-element.382), channel_id=1, source_target_pairs={{0,4},{4,8},{8,12},{1,5},{5,9},{9,13},{2,6},{6,10},{10,14},{3,7},{... | collective-permute-start | bytes 49160 | tf_op jit(solution)/shard_map/while/body/eval_jaxpr/ppermute | solution.py:12
  230.0 3.4 %collective-permute-start.2 = (bf16[1,10,1,8,128]{4,3,2,1,0:T(8,128)(2,1)S(1)}, bf16[1,10,1,8,128]{4,3,2,1,0:T(8,128)(2,1)S(1)}, u32[]{:S(2)}, u32[]{:S(2)}) collective-permute-start(bf16[1,10,1,8,128]{4,3,2,1,0:T(8,128)(2,1)S(1)} %get-tuple-element.383), channel_id=1, source_target_pairs={{1,0},{2,1},{3,2},{5,4},{6,5},{7,6},{9,8},{10,9},{11,10},{13,12},{... | collective-permute-start | bytes 61448 | tf_op jit(solution)/shard_map/while/body/eval_jaxpr/ppermute | solution.py:15
  231.9 5.7 %collective-permute-start.3 = (bf16[1,10,1,8,128]{4,3,2,1,0:T(8,128)(2,1)S(1)}, bf16[1,10,1,8,128]{4,3,2,1,0:T(8,128)(2,1)S(1)}, u32[]{:S(2)}, u32[]{:S(2)}) collective-permute-start(bf16[1,10,1,8,128]{4,3,2,1,0:T(8,128)(2,1)S(1)} %get-tuple-element.384), channel_id=1, source_target_pairs={{0,1},{1,2},{2,3},{4,5},{5,6},{6,7},{8,9},{9,10},{10,11},{12,13},{... | collective-permute-start | bytes 61448 | tf_op jit(solution)/shard_map/while/body/eval_jaxpr/ppermute | solution.py:12
  241.2 6.9 %collective-permute-start.4 = (bf16[1,8,8,8,128]{4,3,2,1,0:T(8,128)(2,1)S(1)}, bf16[1,8,8,8,128]{4,3,2,1,0:T(8,128)(2,1)S(1)}, u32[]{:S(2)}, u32[]{:S(2)}) collective-permute-start(bf16[1,8,8,8,128]{4,3,2,1,0:T(8,128)(2,1)S(1)} %get-tuple-element.395), channel_id=1, source_target_pairs={{0,16},{1,17},{2,18},{3,19},{4,20},{5,21},{6,22},{7,23},{8,24},{9,... | collective-permute-start | bytes 393224 | tf_op jit(solution)/shard_map/while/body/eval_jaxpr/ppermute | solution.py:23
  248.0 1.0 copy-start.1
where the time goes:
time: 251 us; the launch traced here: 249 us
  waiting for transfers between devices  111 us (44%)
  starting transfers between devices  80.8 us (32%)
  other arithmetic  31.3 us (12%)
  matrix products  19.7 us (8%)
  local copies, waits for them, and re-layouts  3.11 us (1%)
    ppermute x18, waiting for transfers between devices, extended(): lax.ppermute(lax.slice_in_dim(block, block.shape[dim] - width, None, axis...  61.4 us
    ppermute x9, waiting for transfers between devices, from_behind(): return lax.ppermute(array, axis, pairs)  50 us
    ppermute x18, starting transfers between devices, extended(): lax.ppermute(lax.slice_in_dim(block, 0, width, axis=dim), axis, backward)  35.9 us
    ppermute x18, starting transfers between devices, extended(): lax.ppermute(lax.slice_in_dim(block, block.shape[dim] - width, None, axis...  33.3 us
    dot_general x81, matrix products, denoise(): jnp.dot(shifted_view.reshape(-1, channels), spatial[tap_index], preferred...  13.7 us
    ppermute x9, starting transfers between devices, from_behind(): return lax.ppermute(array, axis, pairs)  11.6 us
    reduce_sum x9, other arithmetic, denoise(): jnp.mean(noisy * noisy, axis=-1, keepdims=True) + 1e-05  10.1 us
    convert_element_type x9, other arithmetic, denoise(): normalized = (noisy * lax.rsqrt(jnp.mean(noisy * noisy, axis=-1, keepdims...  9.38 us
  transfers between devices with their start and end apart: 45, of which 27 were waited for; matrix products, arithmetic and copies ran while one was open for 1% of the time, Pallas kernels for 0%

commit v1 on v0

v1 whole, which is shorter than its diff:
```python
import functools

import jax
import jax.numpy as jnp
from jax import lax
from jax.experimental import pallas as pl
from jax.experimental.pallas import tpu as pltpu
from jax.sharding import PartitionSpec as P

MESH = pl.DeviceIdType.MESH
SIDES = (("frames", 1), ("frames", -1), ("space", 1), ("space", -1))
CHUNK = 4


def kernel(
    videos, frames, rows, cols, channels,
    level_ref, base_hbm, noise_hbm, spatial_hbm, temporal_hbm, output_hbm, out_hbm,
    noise, prior, result, weights, noisy_ref, middle, before, after, edge_out, edge_in,
    noise_sem, base_sem, weight_sem, store_sem, chain_send, chain_recv, edge_send, edge_recv,
):
    place = {axis: lax.axis_index(axis) for axis in ("section", "frames", "space")}
    count = {axis: lax.axis_size(axis) for axis in place}

    def has(axis, step):
        return place[axis] < count[axis] - 1 if step > 0 else place[axis] > 0

    def peer(axis, step):
        return {axis: lax.rem(place[axis] + step + count[axis], count[axis])}

    first = place["section"] == 0
    onward = has("section", 1)

    def load_noise(v):
        return pltpu.make_async_copy(noise_hbm.at[v], noise.at[v], noise_sem.at[v])

    def load_base(v):
        return pltpu.make_async_copy(base_hbm.at[v], prior.at[v], base_sem.at[v])

    def store(v):
        return pltpu.make_async_copy(result.at[v], out_hbm.at[v], store_sem.at[v])

    def pass_on(v):
        return pltpu.make_async_remote_copy(
            src_ref=result.at[v], dst_ref=prior.at[v],
            send_sem=chain_send.at[v], recv_sem=chain_recv.at[v],
            device_id=peer("section", 1), device_id_type=MESH,
        )

    def edge(d, v):
        return pltpu.make_async_remote_copy(
            src_ref=edge_out.at[d, v], dst_ref=edge_in.at[d, v],
            send_sem=edge_send.at[d, v], recv_sem=edge_recv.at[d, v],
            device_id=peer(*SIDES[d]), device_id_type=MESH,
        )

    weight_loads = [
        pltpu.make_async_copy(spatial_hbm, weights.at[pl.ds(0, 9)], weight_sem.at[0]),
        pltpu.make_async_copy(temporal_hbm, weights.at[pl.ds(9, 3)], weight_sem.at[1]),
        pltpu.make_async_copy(output_hbm, weights.at[pl.ds(12, 1)], weight_sem.at[2]),
    ]

    neighbours = SIDES + (("section", 1), ("section", -1))
    barrier = pltpu.get_barrier_semaphore()
    for axis, step in neighbours:
        @pl.when(has(axis, step))
        def _():
            pl.semaphore_signal(barrier, inc=1, device_id=peer(axis, step), device_id_type=MESH)

    @pl.loop(0, videos)
    def _(v):
        load_noise(v).start()

        @pl.when(first)
        def _():
            load_base(v).start()

    for copy in weight_loads:
        copy.start()

    for d, (axis, step) in enumerate(SIDES):
        @pl.when(jnp.logical_not(has(axis, -step)))
        def _():
            edge_in[d] = jnp.zeros(edge_in.shape[1:], edge_in.dtype)

    pl.semaphore_wait(barrier, sum(has(*side).astype(jnp.int32) for side in neighbours))

    level = level_ref[...].astype(jnp.float32)

    def spread(v, x, at, size):
        lines = x.shape[0] * x.shape[1]
        flat = x.reshape(lines, cols, channels)
        column = lax.broadcasted_iota(jnp.int32, flat.shape, 1)
        left = jnp.where(column == 0, 0.0, pltpu.roll(flat, 1, 1))
        right = jnp.where(column == cols - 1, 0.0, pltpu.roll(flat, cols - 1, 1))
        middle[v, 1 : 1 + frames, at : at + size] = x
        before[v, :, at : at + size] = left.reshape(x.shape)
        after[v, :, at : at + size] = right.reshape(x.shape)

    def prepare(v):
        load_noise(v).wait()

        @pl.when(first)
        def _():
            load_base(v).wait()

        @pl.when(jnp.logical_not(first))
        def _():
            pass_on(v).wait_recv()

        noisy = prior[v].astype(jnp.float32) + level * noise[v].astype(jnp.float32)
        noisy_ref[v] = noisy
        power = jnp.mean(noisy * noisy, axis=-1, keepdims=True)
        normalized = (noisy * lax.rsqrt(power + 1e-05)).astype(jnp.bfloat16)
        x = normalized.astype(jnp.float32).reshape(frames, rows, cols, channels)
        edge_out[0, v] = normalized[frames - 1]
        edge_out[1, v] = normalized[0]
        edge_out[2, v] = x[:, rows - 1].reshape(frames * cols, channels).astype(jnp.bfloat16)
        edge_out[3, v] = x[:, 0].reshape(frames * cols, channels).astype(jnp.bfloat16)
        for d, side in enumerate(SIDES):
            @pl.when(has(*side))
            def _():
                edge(d, v).start()
        spread(v, x, 1, rows)

    def convolve(v):
        for d, (axis, step) in enumerate(SIDES):
            @pl.when(has(axis, -step))
            def _():
                edge(d, v).wait_recv()
        middle[v, 0, 1 : 1 + rows] = edge_in[0, v].astype(jnp.float32).reshape(rows, cols, channels)
        middle[v, frames + 1, 1 : 1 + rows] = (
            edge_in[1, v].astype(jnp.float32).reshape(rows, cols, channels)
        )
        for d, at in ((2, 0), (3, rows + 1)):
            spread(v, edge_in[d, v].astype(jnp.float32).reshape(frames, 1, cols, channels), at, 1)
        kernel_matrix = weights[0:12].reshape(12 * channels, channels)
        for f in range(0, frames, CHUNK):
            taps = []
            for a in range(3):
                for ref, skip in ((before, 0), (middle, 1), (after, 0)):
                    taps.append(ref[v, f + skip : f + skip + CHUNK, a : a + rows])
            for t in range(3):
                taps.append(middle[v, f + t : f + t + CHUNK, 1 : 1 + rows])
            taps = [tap.reshape(-1, channels).astype(jnp.bfloat16) for tap in taps]
            pre = jnp.dot(
                jnp.concatenate(taps, axis=-1), kernel_matrix, preferred_element_type=jnp.float32
            )
            activated = (pre / (1.0 + jnp.exp(-pre))).astype(jnp.bfloat16)
            estimate = jnp.dot(activated, weights[12], preferred_element_type=jnp.float32)
            held = noisy_ref[v, f : f + CHUNK]
            result[v, f : f + CHUNK] = (held - level * estimate.reshape(held.shape)).astype(
                jnp.bfloat16
            )

        @pl.when(onward)
        def _():
            pass_on(v).start()

        store(v).start()

    @pl.loop(0, videos + 1)
    def _(i):
        @pl.when(i < videos)
        def _():
            prepare(i)

        @pl.when(i == 1)
        def _():
            for copy in weight_loads:
                copy.wait()

        @pl.when(i > 0)
        def _():
            convolve(i - 1)

    @pl.loop(0, videos)
    def _(v):
        store(v).wait()

        @pl.when(onward)
        def _():
            pass_on(v).wait_send()

        for d, side in enumerate(SIDES):
            @pl.when(has(*side))
            def _():
                edge(d, v).wait_send()


def on_device(
    base_frames, section_noise, noise_levels, spatial_kernel, temporal_kernel, output_weight
):
    videos, frames, rows, cols, channels = base_frames.shape
    flat = (videos, frames, rows * cols, channels)
    wide = (videos, frames, rows + 2, cols, channels)
    edges = (len(SIDES), videos, frames * cols, channels)
    assert frames == rows and frames % CHUNK == 0
    result = pl.pallas_call(
        functools.partial(kernel, videos, frames, rows, cols, channels),
        out_shape=jax.ShapeDtypeStruct(flat, jnp.bfloat16),
        in_specs=[pl.BlockSpec(memory_space=pltpu.VMEM)] + [pl.BlockSpec(memory_space=pl.ANY)] * 5,
        out_specs=pl.BlockSpec(memory_space=pl.ANY),
        scratch_shapes=[
            pltpu.VMEM(flat, jnp.bfloat16),
            pltpu.VMEM(flat, jnp.bfloat16),
            pltpu.VMEM(flat, jnp.bfloat16),
            pltpu.VMEM((13, channels, channels), jnp.bfloat16),
            pltpu.VMEM(flat, jnp.float32),
            pltpu.VMEM((videos, frames + 2, rows + 2, cols, channels), jnp.float32),
            pltpu.VMEM(wide, jnp.float32),
            pltpu.VMEM(wide, jnp.float32),
            pltpu.VMEM(edges, jnp.bfloat16),
            pltpu.VMEM(edges, jnp.bfloat16),
            pltpu.SemaphoreType.DMA((videos,)),
            pltpu.SemaphoreType.DMA((videos,)),
            pltpu.SemaphoreType.DMA((3,)),
            pltpu.SemaphoreType.DMA((videos,)),
            pltpu.SemaphoreType.DMA((videos,)),
            pltpu.SemaphoreType.DMA((videos,)),
            pltpu.SemaphoreType.DMA((len(SIDES), videos)),
            pltpu.SemaphoreType.DMA((len(SIDES), videos)),
        ],
        compiler_params=pltpu.CompilerParams(
            collective_id=0, has_side_effects=True, vmem_limit_bytes=40 * 2**20
        ),
    )(
        noise_levels.reshape(1, 1),
        base_frames.reshape(flat),
        section_noise.reshape(flat),
        spatial_kernel[0],
        temporal_kernel[0],
        output_weight,
    )
    return result.reshape((1,) + base_frames.shape)


def solution(mesh):
    return jax.shard_map(
        on_device,
        mesh=mesh,
        in_specs=(
            P(None, "frames", "space", None, None),
            P("section", None, "frames", "space", None, None),
            P("section"),
            P("section", None, None, None),
            P("section", None, None, None),
            P("section", None, None),
        ),
        out_specs=P("section", None, "frames", "space", None, None),
        check_vma=False,
    )
```

time: 251 us -> 43.7 us (0.17)
  the two profiles are of different devices: /device:TPU:30 before, /device:TPU:2 now
where the time goes in v1:
time: 43.7 us; the launch traced here: 43.4 us
  Pallas kernels  36.7 us (84%)
  local copies, waits for them, and re-layouts  6.03 us (14%)
  between operations  0.68 us (2%)
    pallas_call x1, Pallas kernels, on_device(): pl.pallas_call(functools.partial(kernel, videos, frames, rows, cols, chan...  36.7 us
    unnamed x11, local copies, waits for them, and re-layouts  6.03 us

profile of v1, /device:TPU:2, one launch (start us, length us, event | category | flops | bytes accessed | tf_op | source)
XLA Modules:
  0.0 43.4 jit_solution(475718236163470287)
XLA Ops:
  0.7 0.0 copy-start
  0.7 1.2 %copy-done = bf16[8,8,8,8,128]{4,3,2,1,0:T(8,128)(2,1)S(1)} copy-done((bf16[8,8,8,8,128]{4,3,2,1,0:T(8,128)(2,1)S(1)}, bf16[8,8,8,8,128]{4,3,2,1,0:T(8,128)(2,1)}, u32[]{:S(2)}) %copy-start) | copy-done | bytes 1048600
  1.9 0.0 copy-start.1
  1.9 1.2 %copy-done.1 = bf16[1,8,8,8,8,128]{5,4,3,2,1,0:T(8,128)(2,1)S(1)} copy-done((bf16[1,8,8,8,8,128]{5,4,3,2,1,0:T(8,128)(2,1)S(1)}, bf16[1,8,8,8,8,128]{5,4,3,2,1,0:T(8,128)(2,1)}, u32[]{:S(2)}) %copy-start.1) | copy-done | bytes 1048600
  3.1 0.0 copy-start.2
  3.1 1.0 %copy-done.2 = bf16[1,9,128,128]{3,2,1,0:T(8,128)(2,1)S(1)} copy-done((bf16[1,9,128,128]{3,2,1,0:T(8,128)(2,1)S(1)}, bf16[1,9,128,128]{3,2,1,0:T(8,128)(2,1)}, u32[]{:S(2)}) %copy-start.2) | copy-done | bytes 294936
  4.1 0.0 copy-start.3
  4.1 0.9 %copy-done.3 = bf16[1,3,128,128]{3,2,1,0:T(8,128)(2,1)S(1)} copy-done((bf16[1,3,128,128]{3,2,1,0:T(8,128)(2,1)S(1)}, bf16[1,3,128,128]{3,2,1,0:T(8,128)(2,1)}, u32[]{:S(2)}) %copy-start.3) | copy-done | bytes 98328
  5.0 0.0 copy-start.4
  5.0 0.8 %copy-done.4 = bf16[1,128,128]{2,1,0:T(8,128)(2,1)S(1)} copy-done((bf16[1,128,128]{2,1,0:T(8,128)(2,1)S(1)}, bf16[1,128,128]{2,1,0:T(8,128)(2,1)}, u32[]{:S(2)}) %copy-start.4) | copy-done | bytes 32792
  5.7 36.7 %shard_map.64 = bf16[8,8,64,128]{3,2,1,0:T(8,128)(2,1)S(1)} custom-call(bf16[1,1]{1,0:T(2,128)(2,1)} %bitcast.6.level_ref, bf16[8,8,64,128]{3,2,1,0:T(8,128)(2,1)S(1)} %bitcast.8, bf16[8,8,64,128]{3,2,1,0:T(8,128)(2,1)S(1)} %bitcast.9, bf16[9,128,128]{2,1,0:T(8,128)(2,1)S(1)} %bitcast.10, bf16[3,128,128]{2,1,0:T(8,128)(2,1)S(1)} %bitcast.11, ...), custom_call_target="tpu_custom_call" | custom-call | tf_op jit(solution)/shard_map/pallas_call | solution.py:198
  42.4 1.0 %copy.9 = bf16[1,8,8,8,8,128]{5,4,3,2,1,0:T(8,128)(2,1)} copy(bf16[1,8,8,8,8,128]{5,4,3,2,1,0:T(8,128)(2,1)S(1)} %bitcast.7) | data formatting | bytes 2097152
Async XLA Ops:
  0.7 1.2 %copy-start = (bf16[8,8,8,8,128]{4,3,2,1,0:T(8,128)(2,1)S(1)}, bf16[8,8,8,8,128]{4,3,2,1,0:T(8,128)(2,1)}, u32[]{:S(2)}) copy-start(bf16[8,8,8,8,128]{4,3,2,1,0:T(8,128)(2,1)} %param.6) | copy-start | bytes 3145732
  1.9 1.2 %copy-start.1 = (bf16[1,8,8,8,8,128]{5,4,3,2,1,0:T(8,128)(2,1)S(1)}, bf16[1,8,8,8,8,128]{5,4,3,2,1,0:T(8,128)(2,1)}, u32[]{:S(2)}) copy-start(bf16[1,8,8,8,8,128]{5,4,3,2,1,0:T(8,128)(2,1)} %param.7) | copy-start | bytes 3145732
  3.1 1.0 %copy-start.2 = (bf16[1,9,128,128]{3,2,1,0:T(8,128)(2,1)S(1)}, bf16[1,9,128,128]{3,2,1,0:T(8,128)(2,1)}, u32[]{:S(2)}) copy-start(bf16[1,9,128,128]{3,2,1,0:T(8,128)(2,1)} %param.9) | copy-start | bytes 884740
  4.1 0.9 %copy-start.3 = (bf16[1,3,128,128]{3,2,1,0:T(8,128)(2,1)S(1)}, bf16[1,3,128,128]{3,2,1,0:T(8,128)(2,1)}, u32[]{:S(2)}) copy-start(bf16[1,3,128,128]{3,2,1,0:T(8,128)(2,1)} %param.10) | copy-start | bytes 294916
  5.0 0.8 %copy-start.4 = (bf16[1,128,128]{2,1,0:T(8,128)(2,1)S(1)}, bf16[1,128,128]{2,1,0:T(8,128)(2,1)}, u32[]{:S(2)}) copy-start(bf16[1,128,128]{2,1,0:T(8,128)(2,1)} %output_hbm.1) | copy-start | bytes 98308

commit v2 on v1

v2 whole, which is shorter than its diff:
```python
import functools

import jax
import jax.numpy as jnp
from jax import lax
from jax.experimental import pallas as pl
from jax.experimental.pallas import tpu as pltpu
from jax.sharding import PartitionSpec as P

MESH = pl.DeviceIdType.MESH
SIDES = (("frames", 1), ("frames", -1), ("space", 1), ("space", -1))
CHUNK = 4


def kernel(
    videos, ahead, frames, rows, cols, channels,
    level_ref, base_hbm, noise_hbm, spatial_hbm, temporal_hbm, output_hbm, out_hbm,
    noise, prior, result, weights, levels, level_out, level_in,
    noisy_ref, middle, before, after, edge_out, edge_in,
    noise_sem, base_sem, weight_sem, store_sem, chain_send, chain_recv, edge_send, edge_recv,
    lend_send, lend_recv,
):
    place = {axis: lax.axis_index(axis) for axis in ("section", "frames", "space")}
    count = {axis: lax.axis_size(axis) for axis in place}

    def has(axis, step):
        return place[axis] < count[axis] - 1 if step > 0 else place[axis] > 0

    def peer(axis, step):
        return {axis: lax.rem(place[axis] + step + count[axis], count[axis])}

    first = place["section"] == 0
    later = jnp.logical_not(first)
    onward = has("section", 1)
    items = videos + ahead
    lag = ahead + 1

    def special(v):
        return jnp.logical_and(v >= videos - lag, v < videos - 1) if ahead else False

    def active(j):
        if not ahead:
            return j < videos
        usual = jnp.logical_and(j < videos, jnp.logical_not(special(j)))
        return jnp.logical_or(usual, jnp.logical_and(first, j < items))

    def load_noise(v):
        return pltpu.make_async_copy(noise_hbm.at[v], noise.at[v], noise_sem.at[v])

    def load_base(v):
        return pltpu.make_async_copy(base_hbm.at[v], prior.at[v], base_sem.at[v])

    def store(v):
        return pltpu.make_async_copy(result.at[v], out_hbm.at[v], store_sem.at[v])

    def pass_on(v):
        return pltpu.make_async_remote_copy(
            src_ref=result.at[v], dst_ref=prior.at[v],
            send_sem=chain_send.at[v], recv_sem=chain_recv.at[v],
            device_id=peer("section", 1), device_id_type=MESH,
        )

    def finish(j):
        return pltpu.make_async_remote_copy(
            src_ref=result.at[j], dst_ref=out_hbm.at[j - lag],
            send_sem=chain_send.at[j], recv_sem=chain_recv.at[j],
            device_id=peer("section", 1), device_id_type=MESH,
        )

    def edge(d, v):
        return pltpu.make_async_remote_copy(
            src_ref=edge_out.at[d, v], dst_ref=edge_in.at[d, v],
            send_sem=edge_send.at[d, v], recv_sem=edge_recv.at[d, v],
            device_id=peer(*SIDES[d]), device_id_type=MESH,
        )

    parts = ((spatial_hbm, 0, 9), (temporal_hbm, 9, 3), (output_hbm, 12, 1))
    weight_loads = [
        pltpu.make_async_copy(source, weights.at[0, pl.ds(at, size)], weight_sem.at[n])
        for n, (source, at, size) in enumerate(parts)
    ]
    loans = []
    if ahead:
        pairs = [(level_out, level_in)]
        pairs += [(source, weights.at[1, pl.ds(at, size)]) for source, at, size in parts]
        for v in range(videos - lag, videos - 1):
            pairs.append((noise_hbm.at[v], noise.at[v + lag]))
        loans = [
            pltpu.make_async_remote_copy(
                src_ref=source, dst_ref=target, send_sem=lend_send.at[n], recv_sem=lend_recv.at[n],
                device_id=peer("section", -1), device_id_type=MESH,
            )
            for n, (source, target) in enumerate(pairs)
        ]

    def passes(v):
        if not ahead:
            return onward
        return jnp.logical_and(onward, jnp.logical_and(v < videos, jnp.logical_not(special(v))))

    neighbours = SIDES + (("section", 1), ("section", -1))
    barrier = pltpu.get_barrier_semaphore()
    for axis, step in neighbours:
        @pl.when(has(axis, step))
        def _():
            pl.semaphore_signal(barrier, inc=1, device_id=peer(axis, step), device_id_type=MESH)

    @pl.loop(0, videos)
    def _(v):
        @pl.when(active(v))
        def _():
            load_noise(v).start()

        @pl.when(first)
        def _():
            load_base(v).start()

    for copy in weight_loads:
        copy.start()

    for d, (axis, step) in enumerate(SIDES):
        @pl.when(jnp.logical_not(has(axis, -step)))
        def _():
            edge_in[d] = jnp.zeros(edge_in.shape[1:], edge_in.dtype)

    levels[0] = jnp.broadcast_to(level_ref[...].astype(jnp.float32), levels.shape[1:])
    level_out[...] = jnp.broadcast_to(level_ref[...], level_out.shape)

    def spread(v, x, at, size):
        lines = x.shape[0] * x.shape[1]
        flat = x.reshape(lines, cols, channels)
        column = lax.broadcasted_iota(jnp.int32, flat.shape, 1)
        left = jnp.where(column == 0, 0.0, pltpu.roll(flat, 1, 1))
        right = jnp.where(column == cols - 1, 0.0, pltpu.roll(flat, cols - 1, 1))
        middle[v, 1 : 1 + frames, at : at + size] = x
        before[v, :, at : at + size] = left.reshape(x.shape)
        after[v, :, at : at + size] = right.reshape(x.shape)

    def normalise(v, number):
        noisy = prior[v].astype(jnp.float32) + levels[number][0:1] * noise[v].astype(jnp.float32)
        noisy_ref[v] = noisy
        power = jnp.mean(noisy * noisy, axis=-1, keepdims=True)
        normalized = (noisy * lax.rsqrt(power + 1e-05)).astype(jnp.bfloat16)
        x = normalized.astype(jnp.float32).reshape(frames, rows, cols, channels)
        edge_out[0, v] = normalized[frames - 1]
        edge_out[1, v] = normalized[0]
        edge_out[2, v] = x[:, rows - 1].reshape(frames * cols, channels).astype(jnp.bfloat16)
        edge_out[3, v] = x[:, 0].reshape(frames * cols, channels).astype(jnp.bfloat16)
        spread(v, x, 1, rows)

    def send_edges(v):
        for d, side in enumerate(SIDES):
            @pl.when(has(*side))
            def _():
                edge(d, v).start()

    def prepare(i):
        @pl.when(i < videos)
        def _():
            load_noise(i).wait()

            @pl.when(first)
            def _():
                load_base(i).wait()

            @pl.when(later)
            def _():
                pass_on(i).wait_recv()

        if ahead:
            @pl.when(i == videos)
            def _():
                for copy in loans:
                    copy.wait_recv()
                levels[1] = level_in[0:8].astype(jnp.float32)

            @pl.when(i >= videos)
            def _():
                prior[i] = result[i - lag]

        normalise(i, (i >= videos).astype(jnp.int32) if ahead else 0)

    def convolve(v):
        for d, (axis, step) in enumerate(SIDES):
            @pl.when(has(axis, -step))
            def _():
                edge(d, v).wait_recv()
        number = (v >= videos).astype(jnp.int32) if ahead else 0
        middle[v, 0, 1 : 1 + rows] = edge_in[0, v].astype(jnp.float32).reshape(rows, cols, channels)
        middle[v, frames + 1, 1 : 1 + rows] = (
            edge_in[1, v].astype(jnp.float32).reshape(rows, cols, channels)
        )
        for d, at in ((2, 0), (3, rows + 1)):
            spread(v, edge_in[d, v].astype(jnp.float32).reshape(frames, 1, cols, channels), at, 1)
        kernel_matrix = weights[number, 0:12].reshape(12 * channels, channels)
        projection = weights[number, 12]
        level = levels[number][0:1]
        for f in range(0, frames, CHUNK):
            taps = []
            for a in range(3):
                for ref, skip in ((before, 0), (middle, 1), (after, 0)):
                    taps.append(ref[v, f + skip : f + skip + CHUNK, a : a + rows])
            for t in range(3):
                taps.append(middle[v, f + t : f + t + CHUNK, 1 : 1 + rows])
            taps = [tap.reshape(-1, channels).astype(jnp.bfloat16) for tap in taps]
            pre = jnp.dot(
                jnp.concatenate(taps, axis=-1), kernel_matrix, preferred_element_type=jnp.float32
            )
            activated = (pre / (1.0 + jnp.exp(-pre))).astype(jnp.bfloat16)
            estimate = jnp.dot(activated, projection, preferred_element_type=jnp.float32)
            held = noisy_ref[v, f : f + CHUNK]
            result[v, f : f + CHUNK] = (held - level * estimate.reshape(held.shape)).astype(
                jnp.bfloat16
            )

        @pl.when(passes(v))
        def _():
            pass_on(v).start()

        @pl.when(v < videos)
        def _():
            store(v).start()

        if ahead:
            @pl.when(v >= videos)
            def _():
                finish(v).start()

    @pl.when(first)
    def _():
        load_noise(0).wait()
        load_base(0).wait()
        normalise(0, 0)

    pl.semaphore_wait(barrier, sum(has(*side).astype(jnp.int32) for side in neighbours))

    @pl.when(first)
    def _():
        send_edges(0)

    if ahead:
        @pl.when(later)
        def _():
            for copy in loans:
                copy.start()

    @pl.loop(0, items + 1)
    def _(i):
        @pl.when(jnp.logical_and(active(i), jnp.logical_or(i > 0, later)))
        def _():
            prepare(i)
            send_edges(i)

        @pl.when(i == 1)
        def _():
            for copy in weight_loads:
                copy.wait()

        @pl.when(jnp.logical_and(i > 0, active(i - 1)))
        def _():
            convolve(i - 1)

    @pl.loop(0, items)
    def _(j):
        @pl.when(active(j))
        def _():
            @pl.when(j < videos)
            def _():
                store(j).wait()

            @pl.when(passes(j))
            def _():
                pass_on(j).wait_send()

            if ahead:
                @pl.when(j >= videos)
                def _():
                    finish(j).wait_send()

            for d, side in enumerate(SIDES):
                @pl.when(has(*side))
                def _():
                    edge(d, j).wait_send()

    if ahead:
        @pl.when(later)
        def _():
            for copy in loans:
                copy.wait_send()
            for j in range(videos, items):
                finish(j).wait_recv()


def on_device(
    base_frames, section_noise, noise_levels, spatial_kernel, temporal_kernel, output_weight
):
    videos, frames, rows, cols, channels = base_frames.shape
    ahead = 1 if lax.axis_size("section") == 2 and videos > 2 else 0
    items = videos + ahead
    flat = (frames, rows * cols, channels)
    wide = (items, frames, rows + 2, cols, channels)
    edges = (len(SIDES), items, frames * cols, channels)
    assert frames == rows and frames % CHUNK == 0
    result = pl.pallas_call(
        functools.partial(kernel, videos, ahead, frames, rows, cols, channels),
        out_shape=jax.ShapeDtypeStruct((videos,) + flat, jnp.bfloat16),
        in_specs=[pl.BlockSpec(memory_space=pltpu.VMEM)] + [pl.BlockSpec(memory_space=pl.ANY)] * 5,
        out_specs=pl.BlockSpec(memory_space=pl.ANY),
        scratch_shapes=[
            pltpu.VMEM((items,) + flat, jnp.bfloat16),
            pltpu.VMEM((items,) + flat, jnp.bfloat16),
            pltpu.VMEM((items,) + flat, jnp.bfloat16),
            pltpu.VMEM((1 + ahead, 13, channels, channels), jnp.bfloat16),
            pltpu.VMEM((1 + ahead, 8, channels), jnp.float32),
            pltpu.VMEM((16, channels), jnp.bfloat16),
            pltpu.VMEM((16, channels), jnp.bfloat16),
            pltpu.VMEM((items,) + flat, jnp.float32),
            pltpu.VMEM((items, frames + 2, rows + 2, cols, channels), jnp.float32),
            pltpu.VMEM(wide, jnp.float32),
            pltpu.VMEM(wide, jnp.float32),
            pltpu.VMEM(edges, jnp.bfloat16),
            pltpu.VMEM(edges, jnp.bfloat16),
            pltpu.SemaphoreType.DMA((videos,)),
            pltpu.SemaphoreType.DMA((videos,)),
            pltpu.SemaphoreType.DMA((3,)),
            pltpu.SemaphoreType.DMA((videos,)),
            pltpu.SemaphoreType.DMA((items,)),
            pltpu.SemaphoreType.DMA((items,)),
            pltpu.SemaphoreType.DMA((len(SIDES), items)),
            pltpu.SemaphoreType.DMA((len(SIDES), items)),
            pltpu.SemaphoreType.DMA((4 + videos,)),
            pltpu.SemaphoreType.DMA((4 + videos,)),
        ],
        compiler_params=pltpu.CompilerParams(
            collective_id=0, has_side_effects=True, vmem_limit_bytes=62 * 2**20
        ),
    )(
        noise_levels.reshape(1, 1),
        base_frames.reshape((videos,) + flat),
        section_noise.reshape((videos,) + flat),
        spatial_kernel[0],
        temporal_kernel[0],
        output_weight,
    )
    return result.reshape((1,) + base_frames.shape)


def solution(mesh):
    return jax.shard_map(
        on_device,
        mesh=mesh,
        in_specs=(
            P(None, "frames", "space", None, None),
            P("section", None, "frames", "space", None, None),
            P("section"),
            P("section", None, None, None),
            P("section", None, None, None),
            P("section", None, None),
        ),
        out_specs=P("section", None, "frames", "space", None, None),
        check_vma=False,
    )
```

time: 43.7 us -> 38.5 us (0.88)
  local copies, waits for them, and re-layouts: 6.03 us -> 2.26 us
  Pallas kernels: 36.7 us -> 35.1 us
    unnamed x11 -> x1, local copies, waits for them, and re-layouts: 6.03 us -> 2.26 us
    pallas_call x1, Pallas kernels: 36.7 us -> 35.1 us  [on_device(): pl.pallas_call(functools.partial(kernel, videos, ahead, frames, rows, col...]
where the time goes in v2:
time: 38.5 us; the launch traced here: 38.1 us
  Pallas kernels  35.1 us (91%)
  local copies, waits for them, and re-layouts  2.26 us (6%)
  between operations  0.67 us (2%)
    pallas_call x1, Pallas kernels, on_device(): pl.pallas_call(functools.partial(kernel, videos, ahead, frames, rows, col...  35.1 us
    unnamed x1, local copies, waits for them, and re-layouts  2.26 us

profile of v2, /device:TPU:2, one launch (start us, length us, event | category | flops | bytes accessed | tf_op | source)
XLA Modules:
  0.0 38.1 jit_solution(17998059597272398342)
XLA Ops:
  0.7 35.1 %shard_map.64 = bf16[8,8,64,128]{3,2,1,0:T(8,128)(2,1)} custom-call(bf16[1,1]{1,0:T(2,128)(2,1)} %bitcast.6.level_ref, bf16[8,8,64,128]{3,2,1,0:T(8,128)(2,1)} %bitcast.8, bf16[8,8,64,128]{3,2,1,0:T(8,128)(2,1)} %bitcast.9, bf16[9,128,128]{2,1,0:T(8,128)(2,1)} %bitcast.10, bf16[3,128,128]{2,1,0:T(8,128)(2,1)} %bitcast.11, bf16[1,128,128]{2,1,0:T(8,128)(2,1)} %output_hbm.1), custom_call_target="tpu_custom_call" | custom-call | tf_op jit(solution)/shard_map/pallas_call | solution.py:304
  35.8 2.3 %copy.9 = bf16[1,8,8,8,8,128]{5,4,3,2,1,0:T(8,128)(2,1)} copy(bf16[1,8,8,8,8,128]{5,4,3,2,1,0:T(8,128)(2,1)} %bitcast.7) | data formatting | bytes 2097152

commit v3 on v2

--- a/solution.py
+++ b/solution.py
@@ -15,8 +15,8 @@
 def kernel(
     videos, ahead, frames, rows, cols, channels,
     level_ref, base_hbm, noise_hbm, spatial_hbm, temporal_hbm, output_hbm, out_hbm,
-    noise, prior, result, weights, levels, level_out, level_in,
-    noisy_ref, middle, before, after, edge_out, edge_in,
+    noise, prior, result, weights, packed, levels, level_out, level_in,
+    noisy_ref, middle, edge_out, edge_in,
     noise_sem, base_sem, weight_sem, store_sem, chain_send, chain_recv, edge_send, edge_recv,
     lend_send, lend_recv,
 ):
@@ -126,15 +126,16 @@
     levels[0] = jnp.broadcast_to(level_ref[...].astype(jnp.float32), levels.shape[1:])
     level_out[...] = jnp.broadcast_to(level_ref[...], level_out.shape)
 
-    def spread(v, x, at, size):
-        lines = x.shape[0] * x.shape[1]
-        flat = x.reshape(lines, cols, channels)
-        column = lax.broadcasted_iota(jnp.int32, flat.shape, 1)
-        left = jnp.where(column == 0, 0.0, pltpu.roll(flat, 1, 1))
-        right = jnp.where(column == cols - 1, 0.0, pltpu.roll(flat, cols - 1, 1))
-        middle[v, 1 : 1 + frames, at : at + size] = x
-        before[v, :, at : at + size] = left.reshape(x.shape)
-        after[v, :, at : at + size] = right.reshape(x.shape)
+    def pack(number):
+        packed[number] = jnp.zeros(packed.shape[1:], packed.dtype)
+        for a in range(3):
+            line = pl.ds(a * channels, channels)
+            packed[number, 0, line, :channels] = weights[number, 3 * a + 1]
+            packed[number, 0, line, channels:] = weights[number, 3 * a + 2]
+            packed[number, 1, line, :channels] = weights[number, 3 * a]
+        packed[number, 0, 3 * channels :, :channels] = weights[number, 9]
+        packed[number, 1, channels : 2 * channels, channels:] = weights[number, 10]
+        packed[number, 1, 3 * channels :, channels:] = weights[number, 11]
 
     def normalise(v, number):
         noisy = prior[v].astype(jnp.float32) + levels[number][0:1] * noise[v].astype(jnp.float32)
@@ -146,7 +147,7 @@
         edge_out[1, v] = normalized[0]
         edge_out[2, v] = x[:, rows - 1].reshape(frames * cols, channels).astype(jnp.bfloat16)
         edge_out[3, v] = x[:, 0].reshape(frames * cols, channels).astype(jnp.bfloat16)
-        spread(v, x, 1, rows)
+        middle[v, 1 : 1 + frames, 1 : 1 + rows] = x
 
     def send_edges(v):
         for d, side in enumerate(SIDES):
@@ -173,6 +174,7 @@
                 for copy in loans:
                     copy.wait_recv()
                 levels[1] = level_in[0:8].astype(jnp.float32)
+                pack(1)
 
             @pl.when(i >= videos)
             def _():
@@ -191,21 +193,29 @@
             edge_in[1, v].astype(jnp.float32).reshape(rows, cols, channels)
         )
         for d, at in ((2, 0), (3, rows + 1)):
-            spread(v, edge_in[d, v].astype(jnp.float32).reshape(frames, 1, cols, channels), at, 1)
-        kernel_matrix = weights[number, 0:12].reshape(12 * channels, channels)
+            middle[v, 1 : 1 + frames, at] = (
+                edge_in[d, v].astype(jnp.float32).reshape(frames, cols, channels)
+            )
         projection = weights[number, 12]
         level = levels[number][0:1]
+        lines = CHUNK * rows
+        column = lax.broadcasted_iota(jnp.int32, (lines, cols, channels), 1)
         for f in range(0, frames, CHUNK):
-            taps = []
-            for a in range(3):
-                for ref, skip in ((before, 0), (middle, 1), (after, 0)):
-                    taps.append(ref[v, f + skip : f + skip + CHUNK, a : a + rows])
-            for t in range(3):
-                taps.append(middle[v, f + t : f + t + CHUNK, 1 : 1 + rows])
-            taps = [tap.reshape(-1, channels).astype(jnp.bfloat16) for tap in taps]
-            pre = jnp.dot(
-                jnp.concatenate(taps, axis=-1), kernel_matrix, preferred_element_type=jnp.float32
-            )
+            views = [middle[v, f + 1 : f + 1 + CHUNK, a : a + rows] for a in range(3)]
+            views += [middle[v, f + t : f + t + CHUNK, 1 : 1 + rows] for t in (0, 2)]
+            views = [view.reshape(-1, channels).astype(jnp.bfloat16) for view in views]
+            sums = [
+                jnp.dot(
+                    jnp.concatenate(views[:3] + [views[3 + n]], axis=-1), packed[number, n],
+                    preferred_element_type=jnp.float32,
+                )
+                for n in range(2)
+            ]
+            ahead_part = sums[0][:, channels:].reshape(lines, cols, channels)
+            behind_part = sums[1][:, :channels].reshape(lines, cols, channels)
+            shifted = jnp.where(column == cols - 1, 0.0, pltpu.roll(ahead_part, cols - 1, 1))
+            shifted = shifted + jnp.where(column == 0, 0.0, pltpu.roll(behind_part, 1, 1))
+            pre = sums[0][:, :channels] + sums[1][:, channels:] + shifted.reshape(-1, channels)
             activated = (pre / (1.0 + jnp.exp(-pre))).astype(jnp.bfloat16)
             estimate = jnp.dot(activated, projection, preferred_element_type=jnp.float32)
             held = noisy_ref[v, f : f + CHUNK]
@@ -255,6 +265,7 @@
         def _():
             for copy in weight_loads:
                 copy.wait()
+            pack(0)
 
         @pl.when(jnp.logical_and(i > 0, active(i - 1)))
         def _():
@@ -298,26 +309,24 @@
     ahead = 1 if lax.axis_size("section") == 2 and videos > 2 else 0
     items = videos + ahead
     flat = (frames, rows * cols, channels)
-    wide = (items, frames, rows + 2, cols, channels)
     edges = (len(SIDES), items, frames * cols, channels)
     assert frames == rows and frames % CHUNK == 0
     result = pl.pallas_call(
         functools.partial(kernel, videos, ahead, frames, rows, cols, channels),
         out_shape=jax.ShapeDtypeStruct((videos,) + flat, jnp.bfloat16),
-        in_specs=[pl.BlockSpec(memory_space=pltpu.VMEM)] + [pl.BlockSpec(memory_space=pl.ANY)] * 5,
+        in_specs=[pl.BlockSpec(memory_space=pltpu.VMEM)] + [pl.BlockSpec(memory_space=pltpu.HBM)] * 5,
         out_specs=pl.BlockSpec(memory_space=pl.ANY),
         scratch_shapes=[
             pltpu.VMEM((items,) + flat, jnp.bfloat16),
             pltpu.VMEM((items,) + flat, jnp.bfloat16),
             pltpu.VMEM((items,) + flat, jnp.bfloat16),
             pltpu.VMEM((1 + ahead, 13, channels, channels), jnp.bfloat16),
+            pltpu.VMEM((1 + ahead, 2, 4 * channels, 2 * channels), jnp.bfloat16),
             pltpu.VMEM((1 + ahead, 8, channels), jnp.float32),
             pltpu.VMEM((16, channels), jnp.bfloat16),
             pltpu.VMEM((16, channels), jnp.bfloat16),
             pltpu.VMEM((items,) + flat, jnp.float32),
             pltpu.VMEM((items, frames + 2, rows + 2, cols, channels), jnp.float32),
-            pltpu.VMEM(wide, jnp.float32),
-            pltpu.VMEM(wide, jnp.float32),
             pltpu.VMEM(edges, jnp.bfloat16),
             pltpu.VMEM(edges, jnp.bfloat16),
             pltpu.SemaphoreType.DMA((videos,)),
@@ -332,7 +341,7 @@
             pltpu.SemaphoreType.DMA((4 + videos,)),
         ],
         compiler_params=pltpu.CompilerParams(
-            collective_id=0, has_side_effects=True, vmem_limit_bytes=62 * 2**20
+            collective_id=0, has_side_effects=True, vmem_limit_bytes=58 * 2**20
         ),
     )(
         noise_levels.reshape(1, 1),

time: 38.5 us -> 38.1 us (0.990)
  Pallas kernels: 35.1 us -> 34.7 us
    pallas_call x1, Pallas kernels: 35.1 us -> 34.7 us  [on_device(): pl.pallas_call(functools.partial(kernel, videos, ahead, frames, rows, col...]
where the time goes in v3:
time: 38.1 us; the launch traced here: 37.7 us
  Pallas kernels  34.7 us (91%)
  local copies, waits for them, and re-layouts  2.26 us (6%)
  between operations  0.67 us (2%)
    pallas_call x1, Pallas kernels, on_device(): pl.pallas_call(functools.partial(kernel, videos, ahead, frames, rows, col...  34.7 us
    unnamed x1, local copies, waits for them, and re-layouts  2.26 us

profile of v3, /device:TPU:2, one launch (start us, length us, event | category | flops | bytes accessed | tf_op | source)
XLA Modules:
  0.0 37.7 jit_solution(7175718489118939213)
XLA Ops:
  0.7 34.7 %shard_map.64 = bf16[8,8,64,128]{3,2,1,0:T(8,128)(2,1)} custom-call(bf16[1,1]{1,0:T(2,128)(2,1)} %bitcast.6.level_ref, bf16[8,8,64,128]{3,2,1,0:T(8,128)(2,1)} %bitcast.8, bf16[8,8,64,128]{3,2,1,0:T(8,128)(2,1)} %bitcast.9, bf16[9,128,128]{2,1,0:T(8,128)(2,1)} %bitcast.10, bf16[3,128,128]{2,1,0:T(8,128)(2,1)} %bitcast.11, bf16[1,128,128]{2,1,0:T(8,128)(2,1)} %output_hbm.1), custom_call_target="tpu_custom_call" | custom-call | tf_op jit(solution)/shard_map/pallas_call | solution.py:314
  35.4 2.3 %copy.9 = bf16[1,8,8,8,8,128]{5,4,3,2,1,0:T(8,128)(2,1)} copy(bf16[1,8,8,8,8,128]{5,4,3,2,1,0:T(8,128)(2,1)} %bitcast.7) | data formatting | bytes 2097152

commit v4 on v3

--- a/solution.py
+++ b/solution.py
@@ -14,10 +14,10 @@
 
 def kernel(
     videos, ahead, frames, rows, cols, channels,
-    level_ref, base_hbm, noise_hbm, spatial_hbm, temporal_hbm, output_hbm, out_hbm,
+    level_ref, base_hbm, noise_hbm, spatial_hbm, temporal_hbm, output_hbm, out_ref,
     noise, prior, result, weights, packed, levels, level_out, level_in,
     noisy_ref, middle, edge_out, edge_in,
-    noise_sem, base_sem, weight_sem, store_sem, chain_send, chain_recv, edge_send, edge_recv,
+    noise_sem, base_sem, weight_sem, chain_send, chain_recv, edge_send, edge_recv,
     lend_send, lend_recv,
 ):
     place = {axis: lax.axis_index(axis) for axis in ("section", "frames", "space")}
@@ -49,9 +49,6 @@
 
     def load_base(v):
         return pltpu.make_async_copy(base_hbm.at[v], prior.at[v], base_sem.at[v])
-
-    def store(v):
-        return pltpu.make_async_copy(result.at[v], out_hbm.at[v], store_sem.at[v])
 
     def pass_on(v):
         return pltpu.make_async_remote_copy(
@@ -62,7 +59,7 @@
 
     def finish(j):
         return pltpu.make_async_remote_copy(
-            src_ref=result.at[j], dst_ref=out_hbm.at[j - lag],
+            src_ref=result.at[j], dst_ref=out_ref.at[j - lag],
             send_sem=chain_send.at[j], recv_sem=chain_recv.at[j],
             device_id=peer("section", 1), device_id_type=MESH,
         )
@@ -97,6 +94,12 @@
         if not ahead:
             return onward
         return jnp.logical_and(onward, jnp.logical_and(v < videos, jnp.logical_not(special(v))))
+
+    def sends(v):
+        return jnp.logical_or(passes(v), v >= videos)
+
+    def before(v):
+        return v - 1 - ahead * (v == videos - 1).astype(jnp.int32)
 
     neighbours = SIDES + (("section", 1), ("section", -1))
     barrier = pltpu.get_barrier_semaphore()
@@ -223,18 +226,22 @@
                 jnp.bfloat16
             )
 
+        @pl.when(jnp.logical_and(v > 0, sends(v)))
+        def _():
+            pass_on(before(v)).wait_send()
+
         @pl.when(passes(v))
         def _():
             pass_on(v).start()
-
-        @pl.when(v < videos)
-        def _():
-            store(v).start()
 
         if ahead:
             @pl.when(v >= videos)
             def _():
                 finish(v).start()
+
+        @pl.when(v < videos)
+        def _():
+            out_ref[v] = result[v]
 
     @pl.when(first)
     def _():
@@ -275,23 +282,17 @@
     def _(j):
         @pl.when(active(j))
         def _():
-            @pl.when(j < videos)
-            def _():
-                store(j).wait()
-
-            @pl.when(passes(j))
-            def _():
-                pass_on(j).wait_send()
-
-            if ahead:
-                @pl.when(j >= videos)
-                def _():
-                    finish(j).wait_send()
-
             for d, side in enumerate(SIDES):
                 @pl.when(has(*side))
                 def _():
                     edge(d, j).wait_send()
+
+    @pl.when(onward)
+    def _():
+        if ahead:
+            finish(items - 1).wait_send()
+        else:
+            pass_on(videos - 1).wait_send()
 
     if ahead:
         @pl.when(later)
@@ -313,9 +314,9 @@
     assert frames == rows and frames % CHUNK == 0
     result = pl.pallas_call(
         functools.partial(kernel, videos, ahead, frames, rows, cols, channels),
-        out_shape=jax.ShapeDtypeStruct((videos,) + flat, jnp.bfloat16),
+        out_shape=pltpu.VMEM((videos,) + flat, jnp.bfloat16),
         in_specs=[pl.BlockSpec(memory_space=pltpu.VMEM)] + [pl.BlockSpec(memory_space=pltpu.HBM)] * 5,
-        out_specs=pl.BlockSpec(memory_space=pl.ANY),
+        out_specs=pl.BlockSpec(memory_space=pltpu.VMEM),
         scratch_shapes=[
             pltpu.VMEM((items,) + flat, jnp.bfloat16),
             pltpu.VMEM((items,) + flat, jnp.bfloat16),
@@ -332,7 +333,6 @@
             pltpu.SemaphoreType.DMA((videos,)),
             pltpu.SemaphoreType.DMA((videos,)),
             pltpu.SemaphoreType.DMA((3,)),
-            pltpu.SemaphoreType.DMA((videos,)),
             pltpu.SemaphoreType.DMA((items,)),
             pltpu.SemaphoreType.DMA((items,)),
             pltpu.SemaphoreType.DMA((len(SIDES), items)),

time: 38.1 us -> 39 us (1.024)
  Pallas kernels: 34.7 us -> 37.2 us
  local copies, waits for them, and re-layouts: 2.26 us -> 0.97 us
    pallas_call x1, Pallas kernels: 34.7 us -> 37.2 us  [on_device(): pl.pallas_call(functools.partial(kernel, videos, ahead, frames, rows, col...]
    unnamed x1, local copies, waits for them, and re-layouts: 2.26 us -> 0.97 us
where the time goes in v4:
time: 39 us; the launch traced here: 38.8 us
  Pallas kernels  37.2 us (95%)
  local copies, waits for them, and re-layouts  0.97 us (2%)
  between operations  0.67 us (2%)
    pallas_call x1, Pallas kernels, on_device(): pl.pallas_call(functools.partial(kernel, videos, ahead, frames, rows, col...  37.2 us
    unnamed x1, local copies, waits for them, and re-layouts  0.97 us

profile of v4, /device:TPU:2, one launch (start us, length us, event | category | flops | bytes accessed | tf_op | source)
XLA Modules:
  0.0 38.8 jit_solution(3881006766691744924)
XLA Ops:
  0.7 37.2 %shard_map.64 = bf16[8,8,64,128]{3,2,1,0:T(8,128)(2,1)S(1)} custom-call(bf16[1,1]{1,0:T(2,128)(2,1)} %bitcast.6.level_ref, bf16[8,8,64,128]{3,2,1,0:T(8,128)(2,1)} %bitcast.8, bf16[8,8,64,128]{3,2,1,0:T(8,128)(2,1)} %bitcast.9, bf16[9,128,128]{2,1,0:T(8,128)(2,1)} %bitcast.10, bf16[3,128,128]{2,1,0:T(8,128)(2,1)} %bitcast.11, bf16[1,128,128]{2,1,0:T(8,128)(2,1)} %output_hbm.1), custom_call_target="tpu_custom_call" | custom-call | tf_op jit(solution)/shard_map/pallas_call | solution.py:315
  37.8 1.0 %copy.8 = bf16[1,8,8,8,8,128]{5,4,3,2,1,0:T(8,128)(2,1)} copy(bf16[1,8,8,8,8,128]{5,4,3,2,1,0:T(8,128)(2,1)S(1)} %bitcast.7) | data formatting | bytes 2097152

commit v5 on v4

--- a/solution.py
+++ b/solution.py
@@ -10,6 +10,8 @@
 MESH = pl.DeviceIdType.MESH
 SIDES = (("frames", 1), ("frames", -1), ("space", 1), ("space", -1))
 CHUNK = 4
+DEPTH = 2
+AHEAD = 2
 
 
 def kernel(
@@ -50,17 +52,27 @@
     def load_base(v):
         return pltpu.make_async_copy(base_hbm.at[v], prior.at[v], base_sem.at[v])
 
+    def turn(v):
+        return v - ahead * (v >= videos - 1).astype(jnp.int32) if ahead else v
+
+    def sent(n):
+        return pltpu.make_async_remote_copy(
+            src_ref=result.at[0], dst_ref=prior.at[0],
+            send_sem=chain_send.at[n], recv_sem=chain_recv.at[n],
+            device_id=peer("section", 1), device_id_type=MESH,
+        )
+
     def pass_on(v):
         return pltpu.make_async_remote_copy(
             src_ref=result.at[v], dst_ref=prior.at[v],
-            send_sem=chain_send.at[v], recv_sem=chain_recv.at[v],
+            send_sem=chain_send.at[turn(v)], recv_sem=chain_recv.at[turn(v)],
             device_id=peer("section", 1), device_id_type=MESH,
         )
 
     def finish(j):
         return pltpu.make_async_remote_copy(
             src_ref=result.at[j], dst_ref=out_ref.at[j - lag],
-            send_sem=chain_send.at[j], recv_sem=chain_recv.at[j],
+            send_sem=chain_send.at[j - ahead], recv_sem=chain_recv.at[j - ahead],
             device_id=peer("section", 1), device_id_type=MESH,
         )
 
@@ -97,9 +109,6 @@
 
     def sends(v):
         return jnp.logical_or(passes(v), v >= videos)
-
-    def before(v):
-        return v - 1 - ahead * (v == videos - 1).astype(jnp.int32)
 
     neighbours = SIDES + (("section", 1), ("section", -1))
     barrier = pltpu.get_barrier_semaphore()
@@ -226,9 +235,9 @@
                 jnp.bfloat16
             )
 
-        @pl.when(jnp.logical_and(v > 0, sends(v)))
-        def _():
-            pass_on(before(v)).wait_send()
+        @pl.when(jnp.logical_and(turn(v) >= DEPTH, sends(v)))
+        def _():
+            sent(turn(v) - DEPTH).wait_send()
 
         @pl.when(passes(v))
         def _():
@@ -289,10 +298,8 @@
 
     @pl.when(onward)
     def _():
-        if ahead:
-            finish(items - 1).wait_send()
-        else:
-            pass_on(videos - 1).wait_send()
+        for n in range(max(videos - DEPTH, 0), videos):
+            sent(n).wait_send()
 
     if ahead:
         @pl.when(later)
@@ -307,7 +314,7 @@
     base_frames, section_noise, noise_levels, spatial_kernel, temporal_kernel, output_weight
 ):
     videos, frames, rows, cols, channels = base_frames.shape
-    ahead = 1 if lax.axis_size("section") == 2 and videos > 2 else 0
+    ahead = AHEAD if lax.axis_size("section") == 2 and videos > AHEAD + 1 else 0
     items = videos + ahead
     flat = (frames, rows * cols, channels)
     edges = (len(SIDES), items, frames * cols, channels)

time: 39 us -> 34.2 us (0.88); the launches traced: 38.8 us -> 33.6 us
  Pallas kernels: 37.2 us -> 32 us
    pallas_call x1, Pallas kernels: 37.2 us -> 32 us  [on_device(): pl.pallas_call(functools.partial(kernel, videos, ahead, frames, rows, col...]
where the time goes in v5:
time: 34.2 us; the launch traced here: 33.6 us
  Pallas kernels  32 us (94%)
  local copies, waits for them, and re-layouts  0.97 us (3%)
  between operations  0.67 us (2%)
    pallas_call x1, Pallas kernels, on_device(): pl.pallas_call(functools.partial(kernel, videos, ahead, frames, rows, col...  32 us
    unnamed x1, local copies, waits for them, and re-layouts  0.97 us

profile of v5, /device:TPU:2, one launch (start us, length us, event | category | flops | bytes accessed | tf_op | source)
XLA Modules:
  0.0 33.6 jit_solution(15686439648441713685)
XLA Ops:
  0.7 32.0 %shard_map.64 = bf16[8,8,64,128]{3,2,1,0:T(8,128)(2,1)S(1)} custom-call(bf16[1,1]{1,0:T(2,128)(2,1)} %bitcast.6.level_ref, bf16[8,8,64,128]{3,2,1,0:T(8,128)(2,1)} %bitcast.8, bf16[8,8,64,128]{3,2,1,0:T(8,128)(2,1)} %bitcast.9, bf16[9,128,128]{2,1,0:T(8,128)(2,1)} %bitcast.10, bf16[3,128,128]{2,1,0:T(8,128)(2,1)} %bitcast.11, bf16[1,128,128]{2,1,0:T(8,128)(2,1)} %output_hbm.1), custom_call_target="tpu_custom_call" | custom-call | tf_op jit(solution)/shard_map/pallas_call | solution.py:322
  32.6 1.0 %copy.8 = bf16[1,8,8,8,8,128]{5,4,3,2,1,0:T(8,128)(2,1)} copy(bf16[1,8,8,8,8,128]{5,4,3,2,1,0:T(8,128)(2,1)S(1)} %bitcast.7) | data formatting | bytes 2097152

commit v6 on v5

--- a/solution.py
+++ b/solution.py
@@ -12,15 +12,18 @@
 CHUNK = 4
 DEPTH = 2
 AHEAD = 2
+EARLY = 2
+MARGIN = 16
+PIECES = 5
 
 
 def kernel(
-    videos, ahead, frames, rows, cols, channels,
+    videos, ahead, early, frames, rows, cols, channels,
     level_ref, base_hbm, noise_hbm, spatial_hbm, temporal_hbm, output_hbm, out_ref,
     noise, prior, result, weights, packed, levels, level_out, level_in,
-    noisy_ref, middle, edge_out, edge_in,
+    noisy_ref, middle, edge_out, edge_in, inner,
     noise_sem, base_sem, weight_sem, chain_send, chain_recv, edge_send, edge_recv,
-    lend_send, lend_recv,
+    lend_send, lend_recv, piece_send, piece_recv,
 ):
     place = {axis: lax.axis_index(axis) for axis in ("section", "frames", "space")}
     count = {axis: lax.axis_size(axis) for axis in place}
@@ -66,6 +69,22 @@
         return pltpu.make_async_remote_copy(
             src_ref=result.at[v], dst_ref=prior.at[v],
             send_sem=chain_send.at[turn(v)], recv_sem=chain_recv.at[turn(v)],
+            device_id=peer("section", 1), device_id_type=MESH,
+        )
+
+    def piece(v, n):
+        core = pl.ds(MARGIN, rows * cols - 2 * MARGIN)
+        part = (
+            (pl.ds(1, frames - 2), core),
+            (pl.ds(0, frames), pl.ds(0, MARGIN)),
+            (pl.ds(0, frames), pl.ds(rows * cols - MARGIN, MARGIN)),
+            (pl.ds(0, 1), core),
+            (pl.ds(frames - 1, 1), core),
+        )[n]
+        source = inner if n == 0 else result
+        return pltpu.make_async_remote_copy(
+            src_ref=source.at[v, part[0], part[1]], dst_ref=prior.at[v, part[0], part[1]],
+            send_sem=piece_send.at[v, n], recv_sem=piece_recv.at[v, n],
             device_id=peer("section", 1), device_id_type=MESH,
         )
 
@@ -176,7 +195,19 @@
             def _():
                 load_base(i).wait()
 
-            @pl.when(later)
+            if early:
+                second = place["section"] == 1
+                for v in range(early):
+                    @pl.when(jnp.logical_and(second, i == v))
+                    def _():
+                        for n in range(PIECES):
+                            piece(v, n).wait_recv()
+
+                whole = jnp.logical_or(place["section"] > 1, jnp.logical_and(second, i >= early))
+            else:
+                whole = later
+
+            @pl.when(whole)
             def _():
                 pass_on(i).wait_recv()
 
@@ -194,20 +225,7 @@
 
         normalise(i, (i >= videos).astype(jnp.int32) if ahead else 0)
 
-    def convolve(v):
-        for d, (axis, step) in enumerate(SIDES):
-            @pl.when(has(axis, -step))
-            def _():
-                edge(d, v).wait_recv()
-        number = (v >= videos).astype(jnp.int32) if ahead else 0
-        middle[v, 0, 1 : 1 + rows] = edge_in[0, v].astype(jnp.float32).reshape(rows, cols, channels)
-        middle[v, frames + 1, 1 : 1 + rows] = (
-            edge_in[1, v].astype(jnp.float32).reshape(rows, cols, channels)
-        )
-        for d, at in ((2, 0), (3, rows + 1)):
-            middle[v, 1 : 1 + frames, at] = (
-                edge_in[d, v].astype(jnp.float32).reshape(frames, cols, channels)
-            )
+    def estimate_into(target, v, number):
         projection = weights[number, 12]
         level = levels[number][0:1]
         lines = CHUNK * rows
@@ -231,15 +249,39 @@
             activated = (pre / (1.0 + jnp.exp(-pre))).astype(jnp.bfloat16)
             estimate = jnp.dot(activated, projection, preferred_element_type=jnp.float32)
             held = noisy_ref[v, f : f + CHUNK]
-            result[v, f : f + CHUNK] = (held - level * estimate.reshape(held.shape)).astype(
+            target[v, f : f + CHUNK] = (held - level * estimate.reshape(held.shape)).astype(
                 jnp.bfloat16
             )
 
-        @pl.when(jnp.logical_and(turn(v) >= DEPTH, sends(v)))
+    def convolve(v):
+        for d, (axis, step) in enumerate(SIDES):
+            @pl.when(has(axis, -step))
+            def _():
+                edge(d, v).wait_recv()
+        number = (v >= videos).astype(jnp.int32) if ahead else 0
+        middle[v, 0, 1 : 1 + rows] = edge_in[0, v].astype(jnp.float32).reshape(rows, cols, channels)
+        middle[v, frames + 1, 1 : 1 + rows] = (
+            edge_in[1, v].astype(jnp.float32).reshape(rows, cols, channels)
+        )
+        for d, at in ((2, 0), (3, rows + 1)):
+            middle[v, 1 : 1 + frames, at] = (
+                edge_in[d, v].astype(jnp.float32).reshape(frames, cols, channels)
+            )
+        estimate_into(result, v, number)
+
+        wholes = jnp.where(first, early, 0)
+
+        @pl.when(jnp.logical_and(turn(v) >= DEPTH + wholes, sends(v)))
         def _():
             sent(turn(v) - DEPTH).wait_send()
 
-        @pl.when(passes(v))
+        for w in range(early):
+            @pl.when(jnp.logical_and(first, v == w))
+            def _():
+                for n in range(1, PIECES):
+                    piece(w, n).start()
+
+        @pl.when(jnp.logical_and(passes(v), v >= wholes))
         def _():
             pass_on(v).start()
 
@@ -252,17 +294,33 @@
         def _():
             out_ref[v] = result[v]
 
+    for copy in weight_loads:
+        copy.wait()
+    pack(0)
+
+    def start(v):
+        load_noise(v).wait()
+        load_base(v).wait()
+        normalise(v, 0)
+
     @pl.when(first)
     def _():
-        load_noise(0).wait()
-        load_base(0).wait()
-        normalise(0, 0)
+        start(0)
+        if early:
+            estimate_into(inner, 0, 0)
 
     pl.semaphore_wait(barrier, sum(has(*side).astype(jnp.int32) for side in neighbours))
 
     @pl.when(first)
     def _():
         send_edges(0)
+        if early:
+            piece(0, 0).start()
+        for v in range(1, early):
+            start(v)
+            send_edges(v)
+            estimate_into(inner, v, 0)
+            piece(v, 0).start()
 
     if ahead:
         @pl.when(later)
@@ -272,16 +330,10 @@
 
     @pl.loop(0, items + 1)
     def _(i):
-        @pl.when(jnp.logical_and(active(i), jnp.logical_or(i > 0, later)))
+        @pl.when(jnp.logical_and(active(i), jnp.logical_or(i >= max(early, 1), later)))
         def _():
             prepare(i)
             send_edges(i)
-
-        @pl.when(i == 1)
-        def _():
-            for copy in weight_loads:
-                copy.wait()
-            pack(0)
 
         @pl.when(jnp.logical_and(i > 0, active(i - 1)))
         def _():
@@ -295,6 +347,13 @@
                 @pl.when(has(*side))
                 def _():
                     edge(d, j).wait_send()
+
+    if early:
+        @pl.when(first)
+        def _():
+            for v in range(early):
+                for n in range(PIECES):
+                    piece(v, n).wait_send()
 
     @pl.when(onward)
     def _():
@@ -315,12 +374,14 @@
 ):
     videos, frames, rows, cols, channels = base_frames.shape
     ahead = AHEAD if lax.axis_size("section") == 2 and videos > AHEAD + 1 else 0
+    early = EARLY if lax.axis_size("section") > 1 and videos >= EARLY + DEPTH + ahead else 0
     items = videos + ahead
     flat = (frames, rows * cols, channels)
     edges = (len(SIDES), items, frames * cols, channels)
-    assert frames == rows and frames % CHUNK == 0
+    assert frames == rows and frames % CHUNK == 0 and MARGIN % cols == 0
+    assert rows * cols > 2 * MARGIN and frames > 2
     result = pl.pallas_call(
-        functools.partial(kernel, videos, ahead, frames, rows, cols, channels),
+        functools.partial(kernel, videos, ahead, early, frames, rows, cols, channels),
         out_shape=pltpu.VMEM((videos,) + flat, jnp.bfloat16),
         in_specs=[pl.BlockSpec(memory_space=pltpu.VMEM)] + [pl.BlockSpec(memory_space=pltpu.HBM)] * 5,
         out_specs=pl.BlockSpec(memory_space=pltpu.VMEM),
@@ -337,6 +398,7 @@
             pltpu.VMEM((items, frames + 2, rows + 2, cols, channels), jnp.float32),
             pltpu.VMEM(edges, jnp.bfloat16),
             pltpu.VMEM(edges, jnp.bfloat16),
+            pltpu.VMEM((EARLY,) + flat, jnp.bfloat16),
             pltpu.SemaphoreType.DMA((videos,)),
             pltpu.SemaphoreType.DMA((videos,)),
             pltpu.SemaphoreType.DMA((3,)),
@@ -346,6 +408,8 @@
             pltpu.SemaphoreType.DMA((len(SIDES), items)),
             pltpu.SemaphoreType.DMA((4 + videos,)),
             pltpu.SemaphoreType.DMA((4 + videos,)),
+            pltpu.SemaphoreType.DMA((EARLY, PIECES)),
+            pltpu.SemaphoreType.DMA((EARLY, PIECES)),
         ],
         compiler_params=pltpu.CompilerParams(
             collective_id=0, has_side_effects=True, vmem_limit_bytes=58 * 2**20

time: 34.2 us -> 34.4 us (level)
  no operation moved by 1% of the time
where the time goes in v6:
time: 34.4 us; the launch traced here: 33.8 us
  Pallas kernels  32.2 us (94%)
  local copies, waits for them, and re-layouts  0.97 us (3%)
  between operations  0.67 us (2%)
    pallas_call x1, Pallas kernels, on_device(): pl.pallas_call(functools.partial(kernel, videos, ahead, early, frames, ro...  32.2 us
    unnamed x1, local copies, waits for them, and re-layouts  0.97 us

profile of v6, /device:TPU:2, one launch (start us, length us, event | category | flops | bytes accessed | tf_op | source)
XLA Modules:
  0.0 33.8 jit_solution(4724796862148983835)
XLA Ops:
  0.7 32.2 %shard_map.64 = bf16[8,8,64,128]{3,2,1,0:T(8,128)(2,1)S(1)} custom-call(bf16[1,1]{1,0:T(2,128)(2,1)} %bitcast.6.level_ref, bf16[8,8,64,128]{3,2,1,0:T(8,128)(2,1)} %bitcast.8, bf16[8,8,64,128]{3,2,1,0:T(8,128)(2,1)} %bitcast.9, bf16[9,128,128]{2,1,0:T(8,128)(2,1)} %bitcast.10, bf16[3,128,128]{2,1,0:T(8,128)(2,1)} %bitcast.11, bf16[1,128,128]{2,1,0:T(8,128)(2,1)} %output_hbm.1), custom_call_target="tpu_custom_call" | custom-call | tf_op jit(solution)/shard_map/pallas_call | solution.py:383
  32.8 1.0 %copy.8 = bf16[1,8,8,8,8,128]{5,4,3,2,1,0:T(8,128)(2,1)} copy(bf16[1,8,8,8,8,128]{5,4,3,2,1,0:T(8,128)(2,1)S(1)} %bitcast.7) | data formatting | bytes 2097152

commit v7 on v6

--- a/solution.py
+++ b/solution.py
@@ -12,7 +12,7 @@
 CHUNK = 4
 DEPTH = 2
 AHEAD = 2
-EARLY = 2
+EARLY = 1
 MARGIN = 16
 PIECES = 5
 
@@ -28,11 +28,21 @@
     place = {axis: lax.axis_index(axis) for axis in ("section", "frames", "space")}
     count = {axis: lax.axis_size(axis) for axis in place}
 
+    around = {
+        (axis, step): jnp.clip(place[axis] + step, 0, count[axis] - 1)
+        for axis in place
+        for step in (1, -1)
+    }
+    exists = {
+        (axis, step): place[axis] < count[axis] - 1 if step > 0 else place[axis] > 0
+        for axis, step in around
+    }
+
     def has(axis, step):
-        return place[axis] < count[axis] - 1 if step > 0 else place[axis] > 0
+        return exists[axis, step]
 
     def peer(axis, step):
-        return {axis: lax.rem(place[axis] + step + count[axis], count[axis])}
+        return {axis: around[axis, step]}
 
     first = place["section"] == 0
     later = jnp.logical_not(first)
@@ -246,7 +256,7 @@
             shifted = jnp.where(column == cols - 1, 0.0, pltpu.roll(ahead_part, cols - 1, 1))
             shifted = shifted + jnp.where(column == 0, 0.0, pltpu.roll(behind_part, 1, 1))
             pre = sums[0][:, :channels] + sums[1][:, channels:] + shifted.reshape(-1, channels)
-            activated = (pre / (1.0 + jnp.exp(-pre))).astype(jnp.bfloat16)
+            activated = (0.5 * pre * (1.0 + jnp.tanh(0.5 * pre))).astype(jnp.bfloat16)
             estimate = jnp.dot(activated, projection, preferred_element_type=jnp.float32)
             held = noisy_ref[v, f : f + CHUNK]
             target[v, f : f + CHUNK] = (held - level * estimate.reshape(held.shape)).astype(

time: 34.4 us -> 34.1 us (level)
  Pallas kernels: 32.2 us -> 31.8 us
    pallas_call x1, Pallas kernels: 32.2 us -> 31.8 us  [on_device(): pl.pallas_call(functools.partial(kernel, videos, ahead, early, frames, ro...]
where the time goes in v7:
time: 34.1 us; the launch traced here: 33.5 us
  Pallas kernels  31.8 us (93%)
  local copies, waits for them, and re-layouts  0.97 us (3%)
  between operations  0.67 us (2%)
    pallas_call x1, Pallas kernels, on_device(): pl.pallas_call(functools.partial(kernel, videos, ahead, early, frames, ro...  31.8 us
    unnamed x1, local copies, waits for them, and re-layouts  0.97 us

profile of v7, /device:TPU:2, one launch (start us, length us, event | category | flops | bytes accessed | tf_op | source)
XLA Modules:
  0.0 33.5 jit_solution(3255206241409123166)
XLA Ops:
  0.7 31.8 %shard_map.64 = bf16[8,8,64,128]{3,2,1,0:T(8,128)(2,1)S(1)} custom-call(bf16[1,1]{1,0:T(2,128)(2,1)} %bitcast.6.level_ref, bf16[8,8,64,128]{3,2,1,0:T(8,128)(2,1)} %bitcast.8, bf16[8,8,64,128]{3,2,1,0:T(8,128)(2,1)} %bitcast.9, bf16[9,128,128]{2,1,0:T(8,128)(2,1)} %bitcast.10, bf16[3,128,128]{2,1,0:T(8,128)(2,1)} %bitcast.11, bf16[1,128,128]{2,1,0:T(8,128)(2,1)} %output_hbm.1), custom_call_target="tpu_custom_call" | custom-call | tf_op jit(solution)/shard_map/pallas_call | solution.py:393
  32.5 1.0 %copy.8 = bf16[1,8,8,8,8,128]{5,4,3,2,1,0:T(8,128)(2,1)} copy(bf16[1,8,8,8,8,128]{5,4,3,2,1,0:T(8,128)(2,1)S(1)} %bitcast.7) | data formatting | bytes 2097152

commit v8 on v7

--- a/solution.py
+++ b/solution.py
@@ -12,6 +12,7 @@
 CHUNK = 4
 DEPTH = 2
 AHEAD = 2
+LOOK = 3
 EARLY = 1
 MARGIN = 16
 PIECES = 5
@@ -48,10 +49,11 @@
     later = jnp.logical_not(first)
     onward = has("section", 1)
     items = videos + ahead
-    lag = ahead + 1
+    lag = max(ahead, LOOK) + 1
+    look = jnp.where(first, LOOK, 1)
 
     def special(v):
-        return jnp.logical_and(v >= videos - lag, v < videos - 1) if ahead else False
+        return jnp.logical_and(v >= videos - lag, v < videos - lag + ahead) if ahead else False
 
     def active(j):
         if not ahead:
@@ -66,7 +68,7 @@
         return pltpu.make_async_copy(base_hbm.at[v], prior.at[v], base_sem.at[v])
 
     def turn(v):
-        return v - ahead * (v >= videos - 1).astype(jnp.int32) if ahead else v
+        return v - ahead * (v >= videos - lag + ahead).astype(jnp.int32) if ahead else v
 
     def sent(n):
         return pltpu.make_async_remote_copy(
@@ -121,7 +123,7 @@
     if ahead:
         pairs = [(level_out, level_in)]
         pairs += [(source, weights.at[1, pl.ds(at, size)]) for source, at, size in parts]
-        for v in range(videos - lag, videos - 1):
+        for v in range(videos - lag, videos - lag + ahead):
             pairs.append((noise_hbm.at[v], noise.at[v + lag]))
         loans = [
             pltpu.make_async_remote_copy(
@@ -338,16 +340,16 @@
             for copy in loans:
                 copy.start()
 
-    @pl.loop(0, items + 1)
+    @pl.loop(0, items + LOOK)
     def _(i):
         @pl.when(jnp.logical_and(active(i), jnp.logical_or(i >= max(early, 1), later)))
         def _():
             prepare(i)
             send_edges(i)
 
-        @pl.when(jnp.logical_and(i > 0, active(i - 1)))
-        def _():
-            convolve(i - 1)
+        @pl.when(jnp.logical_and(i >= look, active(i - look)))
+        def _():
+            convolve(i - look)
 
     @pl.loop(0, items)
     def _(j):
@@ -383,8 +385,8 @@
     base_frames, section_noise, noise_levels, spatial_kernel, temporal_kernel, output_weight
 ):
     videos, frames, rows, cols, channels = base_frames.shape
-    ahead = AHEAD if lax.axis_size("section") == 2 and videos > AHEAD + 1 else 0
-    early = EARLY if lax.axis_size("section") > 1 and videos >= EARLY + DEPTH + ahead else 0
+    ahead = AHEAD if lax.axis_size("section") == 2 and videos > max(AHEAD, LOOK) + 1 else 0
+    early = EARLY if lax.axis_size("section") > 1 and videos > EARLY + DEPTH + max(AHEAD, LOOK) else 0
     items = videos + ahead
     flat = (frames, rows * cols, channels)
     edges = (len(SIDES), items, frames * cols, channels)

time: 34.1 us -> 36.9 us (1.082)
  Pallas kernels: 31.8 us -> 34.7 us
    pallas_call x1, Pallas kernels: 31.8 us -> 34.7 us  [on_device(): pl.pallas_call(functools.partial(kernel, videos, ahead, early, frames, ro...]
where the time goes in v8:
time: 36.9 us; the launch traced here: 36.3 us
  Pallas kernels  34.7 us (94%)
  local copies, waits for them, and re-layouts  0.97 us (3%)
  between operations  0.67 us (2%)
    pallas_call x1, Pallas kernels, on_device(): pl.pallas_call(functools.partial(kernel, videos, ahead, early, frames, ro...  34.7 us
    unnamed x1, local copies, waits for them, and re-layouts  0.97 us

profile of v8, /device:TPU:2, one launch (start us, length us, event | category | flops | bytes accessed | tf_op | source)
XLA Modules:
  0.0 36.3 jit_solution(8329846831937737010)
XLA Ops:
  0.7 34.7 %shard_map.64 = bf16[8,8,64,128]{3,2,1,0:T(8,128)(2,1)S(1)} custom-call(bf16[1,1]{1,0:T(2,128)(2,1)} %bitcast.6.level_ref, bf16[8,8,64,128]{3,2,1,0:T(8,128)(2,1)} %bitcast.8, bf16[8,8,64,128]{3,2,1,0:T(8,128)(2,1)} %bitcast.9, bf16[9,128,128]{2,1,0:T(8,128)(2,1)} %bitcast.10, bf16[3,128,128]{2,1,0:T(8,128)(2,1)} %bitcast.11, bf16[1,128,128]{2,1,0:T(8,128)(2,1)} %output_hbm.1), custom_call_target="tpu_custom_call" | custom-call | tf_op jit(solution)/shard_map/pallas_call | solution.py:395
  35.4 1.0 %copy.8 = bf16[1,8,8,8,8,128]{5,4,3,2,1,0:T(8,128)(2,1)} copy(bf16[1,8,8,8,8,128]{5,4,3,2,1,0:T(8,128)(2,1)S(1)} %bitcast.7) | data formatting | bytes 2097152

commit v9 on v8

--- a/solution.py
+++ b/solution.py
@@ -12,7 +12,7 @@
 CHUNK = 4
 DEPTH = 2
 AHEAD = 2
-LOOK = 3
+LOOK = 1
 EARLY = 1
 MARGIN = 16
 PIECES = 5
@@ -183,7 +183,15 @@
     def normalise(v, number):
         noisy = prior[v].astype(jnp.float32) + levels[number][0:1] * noise[v].astype(jnp.float32)
         noisy_ref[v] = noisy
-        power = jnp.mean(noisy * noisy, axis=-1, keepdims=True)
+        square = (noisy * noisy).reshape(-1, channels)
+        high = square.astype(jnp.bfloat16)
+        low = (square - high.astype(jnp.float32)).astype(jnp.bfloat16)
+        total = jnp.dot(
+            jnp.concatenate([high, low], axis=-1),
+            jnp.ones((2 * channels, channels), jnp.bfloat16),
+            preferred_element_type=jnp.float32,
+        )
+        power = total.reshape(noisy.shape) * (1.0 / channels)
         normalized = (noisy * lax.rsqrt(power + 1e-05)).astype(jnp.bfloat16)
         x = normalized.astype(jnp.float32).reshape(frames, rows, cols, channels)
         edge_out[0, v] = normalized[frames - 1]

time: 36.9 us -> 34.5 us (0.935)
  Pallas kernels: 34.7 us -> 32.2 us
    pallas_call x1, Pallas kernels: 34.7 us -> 32.2 us  [on_device(): pl.pallas_call(functools.partial(kernel, videos, ahead, early, frames, ro...]
where the time goes in v9:
time: 34.5 us; the launch traced here: 33.9 us
  Pallas kernels  32.2 us (93%)
  local copies, waits for them, and re-layouts  0.97 us (3%)
  between operations  0.67 us (2%)
    pallas_call x1, Pallas kernels, on_device(): pl.pallas_call(functools.partial(kernel, videos, ahead, early, frames, ro...  32.2 us
    unnamed x1, local copies, waits for them, and re-layouts  0.97 us

profile of v9, /device:TPU:2, one launch (start us, length us, event | category | flops | bytes accessed | tf_op | source)
XLA Modules:
  0.0 33.9 jit_solution(439714667253117020)
XLA Ops:
  0.7 32.2 %shard_map.64 = bf16[8,8,64,128]{3,2,1,0:T(8,128)(2,1)S(1)} custom-call(bf16[1,1]{1,0:T(2,128)(2,1)} %bitcast.6.level_ref, bf16[8,8,64,128]{3,2,1,0:T(8,128)(2,1)} %bitcast.8, bf16[8,8,64,128]{3,2,1,0:T(8,128)(2,1)} %bitcast.9, bf16[9,128,128]{2,1,0:T(8,128)(2,1)} %bitcast.10, bf16[3,128,128]{2,1,0:T(8,128)(2,1)} %bitcast.11, bf16[1,128,128]{2,1,0:T(8,128)(2,1)} %output_hbm.1), custom_call_target="tpu_custom_call" | custom-call | tf_op jit(solution)/shard_map/pallas_call | solution.py:403
  32.9 1.0 %copy.8 = bf16[1,8,8,8,8,128]{5,4,3,2,1,0:T(8,128)(2,1)} copy(bf16[1,8,8,8,8,128]{5,4,3,2,1,0:T(8,128)(2,1)S(1)} %bitcast.7) | data formatting | bytes 2097152

commit v10 on v7

--- a/solution.py
+++ b/solution.py
@@ -9,7 +9,7 @@
 
 MESH = pl.DeviceIdType.MESH
 SIDES = (("frames", 1), ("frames", -1), ("space", 1), ("space", -1))
-CHUNK = 4
+CHUNK = 8
 DEPTH = 2
 AHEAD = 2
 EARLY = 1

time: 34.1 us -> 33.5 us (0.982)
  Pallas kernels: 31.8 us -> 31.2 us
    pallas_call x1, Pallas kernels: 31.8 us -> 31.2 us  [on_device(): pl.pallas_call(functools.partial(kernel, videos, ahead, early, frames, ro...]
where the time goes in v10:
time: 33.5 us; the launch traced here: 32.9 us
  Pallas kernels  31.2 us (93%)
  local copies, waits for them, and re-layouts  0.97 us (3%)
  between operations  0.67 us (2%)
    pallas_call x1, Pallas kernels, on_device(): pl.pallas_call(functools.partial(kernel, videos, ahead, early, frames, ro...  31.2 us
    unnamed x1, local copies, waits for them, and re-layouts  0.97 us

profile of v10, /device:TPU:2, one launch (start us, length us, event | category | flops | bytes accessed | tf_op | source)
XLA Modules:
  0.0 32.9 jit_solution(13811930095232152710)
XLA Ops:
  0.7 31.2 %shard_map.64 = bf16[8,8,64,128]{3,2,1,0:T(8,128)(2,1)S(1)} custom-call(bf16[1,1]{1,0:T(2,128)(2,1)} %bitcast.6.level_ref, bf16[8,8,64,128]{3,2,1,0:T(8,128)(2,1)} %bitcast.8, bf16[8,8,64,128]{3,2,1,0:T(8,128)(2,1)} %bitcast.9, bf16[9,128,128]{2,1,0:T(8,128)(2,1)} %bitcast.10, bf16[3,128,128]{2,1,0:T(8,128)(2,1)} %bitcast.11, bf16[1,128,128]{2,1,0:T(8,128)(2,1)} %output_hbm.1), custom_call_target="tpu_custom_call" | custom-call | tf_op jit(solution)/shard_map/pallas_call | solution.py:393
  31.9 1.0 %copy.8 = bf16[1,8,8,8,8,128]{5,4,3,2,1,0:T(8,128)(2,1)} copy(bf16[1,8,8,8,8,128]{5,4,3,2,1,0:T(8,128)(2,1)S(1)} %bitcast.7) | data formatting | bytes 2097152

commit v11 on v10

--- a/solution.py
+++ b/solution.py
@@ -11,7 +11,7 @@
 SIDES = (("frames", 1), ("frames", -1), ("space", 1), ("space", -1))
 CHUNK = 8
 DEPTH = 2
-AHEAD = 2
+AHEAD = 1
 EARLY = 1
 MARGIN = 16
 PIECES = 5

time: 33.5 us -> 35.9 us (1.072)
  Pallas kernels: 31.2 us -> 33.8 us
    pallas_call x1, Pallas kernels: 31.2 us -> 33.8 us  [on_device(): pl.pallas_call(functools.partial(kernel, videos, ahead, early, frames, ro...]
where the time goes in v11:
time: 35.9 us; the launch traced here: 35.5 us
  Pallas kernels  33.8 us (94%)
  local copies, waits for them, and re-layouts  0.97 us (3%)
  between operations  0.67 us (2%)
    pallas_call x1, Pallas kernels, on_device(): pl.pallas_call(functools.partial(kernel, videos, ahead, early, frames, ro...  33.8 us
    unnamed x1, local copies, waits for them, and re-layouts  0.97 us

profile of v11, /device:TPU:2, one launch (start us, length us, event | category | flops | bytes accessed | tf_op | source)
XLA Modules:
  0.0 35.5 jit_solution(15252927587360503275)
XLA Ops:
  0.7 33.8 %shard_map.64 = bf16[8,8,64,128]{3,2,1,0:T(8,128)(2,1)S(1)} custom-call(bf16[1,1]{1,0:T(2,128)(2,1)} %bitcast.6.level_ref, bf16[8,8,64,128]{3,2,1,0:T(8,128)(2,1)} %bitcast.8, bf16[8,8,64,128]{3,2,1,0:T(8,128)(2,1)} %bitcast.9, bf16[9,128,128]{2,1,0:T(8,128)(2,1)} %bitcast.10, bf16[3,128,128]{2,1,0:T(8,128)(2,1)} %bitcast.11, bf16[1,128,128]{2,1,0:T(8,128)(2,1)} %output_hbm.1), custom_call_target="tpu_custom_call" | custom-call | tf_op jit(solution)/shard_map/pallas_call | solution.py:393
  34.5 1.0 %copy.8 = bf16[1,8,8,8,8,128]{5,4,3,2,1,0:T(8,128)(2,1)} copy(bf16[1,8,8,8,8,128]{5,4,3,2,1,0:T(8,128)(2,1)S(1)} %bitcast.7) | data formatting | bytes 2097152

commit v12 on v10

--- a/solution.py
+++ b/solution.py
@@ -10,7 +10,7 @@
 MESH = pl.DeviceIdType.MESH
 SIDES = (("frames", 1), ("frames", -1), ("space", 1), ("space", -1))
 CHUNK = 8
-DEPTH = 2
+DEPTH = 3
 AHEAD = 2
 EARLY = 1
 MARGIN = 16

time: 33.5 us -> 33.5 us (level)
  no operation moved by 1% of the time
where the time goes in v12:
time: 33.5 us; the launch traced here: 32.9 us
  Pallas kernels  31.2 us (93%)
  local copies, waits for them, and re-layouts  0.97 us (3%)
  between operations  0.67 us (2%)
    pallas_call x1, Pallas kernels, on_device(): pl.pallas_call(functools.partial(kernel, videos, ahead, early, frames, ro...  31.2 us
    unnamed x1, local copies, waits for them, and re-layouts  0.97 us

profile of v12, /device:TPU:2, one launch (start us, length us, event | category | flops | bytes accessed | tf_op | source)
XLA Modules:
  0.0 32.9 jit_solution(12821838007172439582)
XLA Ops:
  0.7 31.2 %shard_map.64 = bf16[8,8,64,128]{3,2,1,0:T(8,128)(2,1)S(1)} custom-call(bf16[1,1]{1,0:T(2,128)(2,1)} %bitcast.6.level_ref, bf16[8,8,64,128]{3,2,1,0:T(8,128)(2,1)} %bitcast.8, bf16[8,8,64,128]{3,2,1,0:T(8,128)(2,1)} %bitcast.9, bf16[9,128,128]{2,1,0:T(8,128)(2,1)} %bitcast.10, bf16[3,128,128]{2,1,0:T(8,128)(2,1)} %bitcast.11, bf16[1,128,128]{2,1,0:T(8,128)(2,1)} %output_hbm.1), custom_call_target="tpu_custom_call" | custom-call | tf_op jit(solution)/shard_map/pallas_call | solution.py:393
  31.9 1.0 %copy.8 = bf16[1,8,8,8,8,128]{5,4,3,2,1,0:T(8,128)(2,1)} copy(bf16[1,8,8,8,8,128]{5,4,3,2,1,0:T(8,128)(2,1)S(1)} %bitcast.7) | data formatting | bytes 2097152
